TPU v7x, 128 devices: a whole 4x4x4 slice. The times are simulated.
128 devices in a mesh: sub: 128 (over z, x, y, core).
Axes of the slice: x: 4, y: 4, z: 4, core: 2. Of those that a mesh axis runs over, the one named last changes fastest.
Arguments:
- load: float32 [16, 256, 512], P(None, 'sub'), may hold values from -6 to 6
- schur_inverse: float32 [256, 512, 512], P('sub'), may hold values from -1 to 2, as said below
- schur: float32 [256, 512, 512], P('sub'), may hold values from -1 to 8, as said below
- corner_map: float32 [256, 24, 512], P('sub'), may hold values from -0.25 to 0.25
- corner_ids: int32 [256, 24], P('sub'), may hold values from 0 to 3071
- coarse_inverse: float32 [3072, 72], P('sub'), may hold values from -1 to 2, as said below
- partner: int32 [256, 512], P('sub'), may hold values from 0 to 131071, as said below
Outputs:
- multipliers: float32 [16, 256, 512], P(None, 'sub')
- residual: float32 [16, 256, 512], P(None, 'sub')
Inputs may be any that keep to these rules, and one draw needn't show every extreme that they name: `schur_inverse`: symmetric positive definite blocks. `schur`: symmetric positive definite blocks. `coarse_inverse`: the matrix that these rows form is symmetric, block tridiagonal over owners and diagonally dominant; the columns of the owner before the first and after the last are zero. `partner`: the pairing is mutual, no dof is paired with itself, and a dof of subdomain s is paired with a dof of a subdomain whose index differs from s by at most 1.
All inputs are finite; a program needn't handle non-finite values.
Results may differ from a plain program's by a relative error of at most 0.0003.
Values sent between devices are 32-bit elements; how exact they have to be, the bound alone decides.
A program may use at most 64 MiB of HBM per device.

v0:
```python
import jax
import jax.numpy as jnp
from jax import lax
from jax.sharding import PartitionSpec as P

ITERS = 2


exact_precision = lax.Precision.HIGHEST


def with_halo(shard, sides, width):
    for axis, dim in sides:
        size, length = (lax.axis_size(axis), shard.shape[dim])
        up = [(i, (i + 1) % size) for i in range(size - 1)]
        down = [(j, i) for i, j in up]
        last = lax.slice_in_dim(shard, length - width, length, axis=dim)
        initial = lax.slice_in_dim(shard, 0, width, axis=dim)
        before = lax.ppermute(last, axis, up)
        after = lax.ppermute(initial, axis, down)
        shard = jnp.concatenate([before, shard, after], axis=dim)
    return shard


def per_device(load, schur_inverse, schur, corner_map, corner_ids, coarse_inverse, partner):
    case_count = load.shape[0]
    sub_count = schur.shape[0]
    dof_count = schur.shape[1]
    owned_count = coarse_inverse.shape[0]
    coarse_count = owned_count * lax.axis_size("sub")
    offset = (lax.axis_index("sub") * sub_count - 1) * dof_count
    local_mate = (partner - offset).reshape(-1)
    corner_flat = corner_ids.reshape(-1)

    def jumped(field):
        padded = with_halo(field, (("sub", 1),), 1)
        flattened = padded.reshape(case_count, -1)
        return field - jnp.take(flattened, local_mate, axis=1).reshape(field.shape)

    def blockwise(matrices, field):
        return jnp.einsum("lsm,smn->lsn", field, matrices, precision=exact_precision)

    def coarse_solve(corner_rows):
        flat_rows = corner_rows.reshape(case_count, -1)
        assembled = (
            jnp.zeros((case_count, coarse_count), jnp.float32).at[:, corner_flat].add(flat_rows)
        )
        owned_rows = lax.psum_scatter(assembled, "sub", scatter_dimension=1, tiled=True)
        window = with_halo(owned_rows[:, None, :], (("sub", 1),), 1).reshape(case_count, -1)
        solved_own = jnp.einsum("lj,ij->li", window, coarse_inverse, precision=exact_precision)
        solved = lax.all_gather(solved_own, "sub", axis=1, tiled=True)
        return jnp.take(solved, corner_flat, axis=1)

    def constrained(field):
        corner_rows = jnp.einsum("lsm,skm->lsk", field, corner_map, precision=exact_precision)
        spread_back = coarse_solve(corner_rows).reshape(case_count, sub_count, -1)
        return blockwise(schur_inverse, field) + jnp.einsum(
            "lsk,skm->lsm", spread_back, corner_map, precision=exact_precision
        )

    def precondition(field):
        return 0.25 * jumped(blockwise(schur, jumped(field)))

    def products(first, second):
        return jnp.sum(first * second, axis=(1, 2))

    def residual_total(residual, smoothed):
        return lax.psum(products(residual, smoothed), "sub")

    residual = jumped(constrained(load))
    multipliers = jnp.zeros_like(residual)
    smoothed = precondition(residual)
    direction = smoothed
    current = residual_total(residual, smoothed)
    for iteration in range(ITERS):
        image = jumped(constrained(jumped(direction)))
        step_length = current / lax.psum(products(direction, image), "sub")
        multipliers = multipliers + step_length[:, None, None] * direction
        residual = residual - step_length[:, None, None] * image
        if iteration + 1 < ITERS:
            smoothed = precondition(residual)
            following = residual_total(residual, smoothed)
            direction = smoothed + (following / current)[:, None, None] * direction
            current = following
    return (multipliers, residual)


def solution(mesh):
    in_specs = (
        P(None, "sub", None),
        P("sub", None, None),
        P("sub", None, None),
        P("sub", None, None),
        P("sub", None),
        P("sub", None),
        P("sub", None),
    )
    out_specs = (P(None, "sub", None), P(None, "sub", None))
    return jax.shard_map(
        per_device, mesh=mesh, in_specs=in_specs, out_specs=out_specs, check_vma=False
    )
```

profile of v0, /device:TPU:1, one launch (start us, length us, event | category | flops | bytes accessed | tf_op | source)
XLA Modules:
  0.0 1176.2 jit_solution(13995161614685904793)
XLA Ops:
  9.4 2.0 scatter_custom_fusion
  12.9 209.8 %reduce-scatter.10.cloned.1.call-done = f32[16,24]{0,1:T(8,128)} async-done(((f32[16,3072]{0,1:T(8,128)}), f32[16,24]{0,1:T(8,128)}) %reduce-scatter.10.cloned.1.call-update) | async-done | bytes 1552
  222.7 4.5 collective-permute-start.1
  231.4 39.5 %all-gather = f32[128,24,16]{1,2,0:T(8,128)S(1)} all-gather(f32[1,24,16]{1,2,0:T(8,128)S(1)} %convolution_bitcast_fusion.9), channel_id=1, replica_groups=mesh['sub'=128] {'sub'}, dimensions={0}, use_global_device_ids=true | all-gather | bytes 198144 | tf_op jit(solution)/shard_map/all_gather | solution.py:51
  272.6 2.0 gather_fusion
  274.9 2.9 collective-permute-start.2
  279.8 3.3 collective-permute-done.3
  283.4 4.0 gather_fusion.1
  290.8 2.4 collective-permute-start.5
  293.2 2.8 collective-permute-done.5
  296.3 4.0 gather_fusion.2
  301.8 2.7 convolution_bitcast_fusion.1
  306.4 2.4 collective-permute-start.7
  308.8 2.8 collective-permute-done.7
  313.5 4.0 gather_fusion.3
  319.0 1.9 collective-permute-start.8
  320.9 2.4 collective-permute-start.9
  323.3 4.1 collective-permute-done.9
  327.8 4.0 gather_fusion.4
  333.6 2.0 scatter_custom_fusion.1
  335.7 222.0 %reduce-scatter.12.cloned.1.call-done = f32[16,24]{0,1:T(8,128)} async-done(((f32[16,3072]{0,1:T(8,128)}), f32[16,24]{0,1:T(8,128)}) %reduce-scatter.12.cloned.1.call-update) | async-done | bytes 1552
  557.7 4.6 collective-permute-start.11
  565.8 39.7 %all-gather.1 = f32[128,24,16]{1,2,0:T(8,128)S(1)} all-gather(f32[1,24,16]{1,2,0:T(8,128)S(1)} %convolution_bitcast_fusion.8), channel_id=1, replica_groups=mesh['sub'=128] {'sub'}, dimensions={0}, use_global_device_ids=true | all-gather | bytes 198144 | tf_op jit(solution)/shard_map/all_gather | solution.py:51
  607.2 2.0 gather_fusion.5
  609.5 2.9 collective-permute-start.12
  614.3 3.3 collective-permute-done.13
  619.5 4.0 gather_fusion.6
  625.1 69.4 %all-reduce.3 = (f32[16]{0:T(128)S(1)}, f32[16]{0:T(128)S(1)}) all-reduce(f32[16]{0:T(128)S(1)} %get-tuple-element.11, f32[16]{0:T(128)S(1)} %get-tuple-element.10), channel_id=1, replica_groups=mesh['sub'=128] {'sub'}, use_global_device_ids=true, to_apply=%region_3.6 | all-reduce | flops 32 | bytes 256 | tf_op jit(solution)/shard_map/psum | solution.py:68
  694.6 3.7 collective-permute-start.14
  700.3 3.3 collective-permute-done.15
  705.5 4.0 gather_fusion.7
  710.9 2.7 convolution_bitcast_fusion
  715.5 2.4 collective-permute-start.17
  717.9 2.8 collective-permute-done.17
  722.7 4.0 gather_fusion.8
  728.2 72.6 %psum.30 = f32[16]{0:T(128)S(1)} all-reduce(f32[16]{0:T(128)S(1)} %multiply_reduce_fusion.1), channel_id=1, replica_groups=mesh['sub'=128] {'sub'}, use_global_device_ids=true, to_apply=%region_9.12 | all-reduce | flops 16 | bytes 128 | tf_op jit(solution)/shard_map/psum | solution.py:68
  800.9 3.8 collective-permute-start.18
  806.6 3.3 collective-permute-done.19
  811.8 4.0 gather_fusion.9
  817.7 2.0 scatter_custom_fusion.2
  819.7 210.8 %reduce-scatter.14.cloned.1.call-done = f32[16,24]{0,1:T(8,128)} async-done(((f32[16,3072]{0,1:T(8,128)}), f32[16,24]{0,1:T(8,128)}) %reduce-scatter.14.cloned.1.call-update) | async-done | bytes 1552
  1030.5 4.6 collective-permute-start.21
  1039.0 39.4 %all-gather.2 = f32[128,24,16]{1,2,0:T(8,128)S(1)} all-gather(f32[1,24,16]{1,2,0:T(8,128)S(1)} %convolution_bitcast_fusion.7), channel_id=1, replica_groups=mesh['sub'=128] {'sub'}, dimensions={0}, use_global_device_ids=true | all-gather | bytes 198144 | tf_op jit(solution)/shard_map/all_gather | solution.py:51
  1080.1 2.0 gather_fusion.10
  1083.2 2.9 collective-permute-start.22
  1088.1 3.3 collective-permute-done.23
  1093.3 4.0 gather_fusion.11
  1098.8 69.4 %psum.31 = f32[16]{0:T(128)S(1)} all-reduce(f32[16]{0:T(128)S(1)} %get-tuple-element.16), channel_id=1, replica_groups=mesh['sub'=128] {'sub'}, use_global_device_ids=true, to_apply=%region_13.16 | all-reduce | flops 16 | bytes 128 | tf_op jit(solution)/shard_map/psum | solution.py:77
  (146 shorter events, 65.4 us)
Async XLA Ops:
  7.2 4.5 copy-start
  7.2 215.5 %reduce-scatter.10.cloned.1.call-start = ((), (), s32[]{:S(2)}) async-start(), calls=%async_computation.3 | async-start | bytes 1585152
  9.4 2.1 copy-start.7
  9.4 2.2 copy-start.6
  9.4 2.2 copy-start.2
  11.4 219.8 %copy-start.3 = (f32[24,72]{1,0:T(8,128)S(1)}, f32[24,72]{1,0:T(8,128)}, u32[]{:S(2)}) copy-start(f32[24,72]{1,0:T(8,128)} %param.16) | copy-start | bytes 20740
  11.4 546.2 %reduce-scatter.12.cloned.1.call-start = ((), (), s32[]{:S(2)}) async-start(), calls=%async_computation.4 | async-start | bytes 1585152
  222.7 6.4 collective-permute-start.1
  227.2 3.3 collective-permute-start
  270.9 3.7 copy-start.1
  274.9 4.8 collective-permute-start.2
  277.8 5.2 collective-permute-start.3
  288.8 4.3 collective-permute-start.4
  290.8 5.2 collective-permute-start.5
  304.5 4.3 collective-permute-start.6
  306.4 5.2 collective-permute-start.7
  319.0 4.3 collective-permute-start.8
  320.9 6.5 collective-permute-start.9
  335.6 694.8 %reduce-scatter.14.cloned.1.call-start = ((), (), s32[]{:S(2)}) async-start(), calls=%async_computation.5 | async-start | bytes 1585152
  557.7 7.9 copy-start.4
  557.7 7.7 collective-permute-start.11
  562.3 3.3 collective-permute-start.10
  609.5 4.8 collective-permute-start.12
  612.4 5.2 collective-permute-start.13
  694.6 5.6 collective-permute-start.14
  698.3 5.2 collective-permute-start.15
  713.6 4.3 collective-permute-start.16
  715.5 5.2 collective-permute-start.17
  800.9 5.8 collective-permute-start.18
  804.7 5.2 collective-permute-start.19
  1030.5 8.3 copy-start.5
  1030.5 8.3 collective-permute-start.21
  1035.1 3.7 collective-permute-start.20
  1083.2 4.8 collective-permute-start.22
  1086.1 5.2 collective-permute-start.23
Sparse Core Ops, SparseCore 0:
  12.7 209.9 reduce-scatter.9
  335.8 221.8 reduce-scatter.11
  819.8 210.6 reduce-scatter.13
where the time goes:
time: 1180 us
  waiting for transfers between devices  673 us (57%)
  blocking collectives  330 us (28%)
  starting transfers between devices  62.7 us (5%)
  local copies, waits for them, and re-layouts  59.8 us (5%)
  other arithmetic  22.8 us (2%)
  between operations  14.5 us (1%)
  matrix products  13.2 us (1%)
    unnamed x6, waiting for transfers between devices  643 us
    psum x2, blocking collectives, residual_total(): return lax.psum(products(residual, smoothed), 'sub')  142 us
    all_gather x3, blocking collectives, coarse_solve(): solved = lax.all_gather(solved_own, 'sub', axis=1, tiled=True)  119 us
    psum x1, blocking collectives, per_device(): step_length = current / lax.psum(products(direction, image), 'sub')  69.4 us
    gather x9, local copies, waits for them, and re-layouts, jumped(): return field - jnp.take(flattened, local_mate, axis=1).reshape(field.shape)  36 us
    ppermute x12, starting transfers between devices, with_halo(): after = lax.ppermute(initial, axis, down)  33 us
    ppermute x12, starting transfers between devices, with_halo(): before = lax.ppermute(last, axis, up)  29.6 us
    ppermute x12, waiting for transfers between devices, with_halo(): after = lax.ppermute(initial, axis, down)  29 us
  transfers between devices with their start and end apart: 27, of which 14 were waited for; matrix products, arithmetic and copies ran while one was open for 0% of the time, Pallas kernels for 0%

commit v1 on v0

v1 whole, which is shorter than its diff:
```python
import functools
import itertools

import jax
import jax.numpy as jnp
from jax import lax
from jax.experimental import pallas as pl
from jax.experimental.pallas import tpu as pltpu
from jax.sharding import PartitionSpec as P

MESH = pl.DeviceIdType.MESH
F32, BF16, I32 = jnp.float32, jnp.bfloat16, jnp.int32
CASES, DOFS, CORNERS, OWN, WIN = 16, 512, 24, 24, 72
LANES = 128
HOPS = (0, 1, 2, 1)

OFFSETS = sorted(
    itertools.product(range(4), range(4), range(4), range(2)),
    key=lambda o: (-(HOPS[o[0]] + HOPS[o[1]] + HOPS[o[2]]), -o[3]),
)
OFFSETS.remove((0, 0, 0, 0))


def split(v):
    high = v.astype(BF16)
    return high, (v - high.astype(F32)).astype(BF16)


def await_bytes(ref, sem):
    pltpu.make_async_copy(ref, ref, sem).wait()


def dot(a, b):
    return jnp.dot(a, b, preferred_element_type=F32)


def take_lanes(values, lanes):
    return jnp.take_along_axis(values, lanes, axis=1, mode="promise_in_bounds")


def iota(shape, dim):
    return lax.broadcasted_iota(I32, shape, dim)


def kernel(
    load_hbm, inverse_hbm, schur_hbm, map_hbm, ids_hbm, coarse_hbm, partner_hbm,
    mult_ref, resid_ref,
    load_v, inverse_v, schur_v, map_v, ids_v, coarse_v, partner_v,
    inv_high, inv_low, sch_high, sch_low, map_high, map_low, map_side,
    table, id_rows, g_high, g_low, field, halo, buf1, buf2, buf3, buf4,
    in_sem, all_send, all_recv, fwd_sem, halo_send, halo_recv,
):
    me = lax.axis_index("sub")
    core, chip = me % 2, me // 2
    y, x, z = chip % 4, chip // 4 % 4, chip // 16
    zs = [(z + i) % 4 * 32 for i in range(4)]
    xs = [(x + i) % 4 * 8 for i in range(4)]
    ys = [(y + i) % 4 * 2 for i in range(4)]
    cs = [core, 1 - core]
    slot = core * 64 + chip
    right, left = (me + 1) % 128, (me + 127) % 128

    def device(o):
        return (zs[o[0]] + xs[o[1]] + ys[o[2]] + cs[o[3]],)

    def slot_of(dev):
        return dev % 2 * 64 + dev // 2

    pairs = (
        (map_hbm, map_v), (load_hbm, load_v), (ids_hbm, ids_v), (coarse_hbm, coarse_v),
        (partner_hbm, partner_v), (inverse_hbm, inverse_v), (schur_hbm, schur_v),
    )
    copies = [pltpu.make_async_copy(a, b, in_sem.at[i]) for i, (a, b) in enumerate(pairs)]
    for copy in copies:
        copy.start()

    barrier = pltpu.get_barrier_semaphore()
    for o in OFFSETS:
        pl.semaphore_signal(barrier, inc=1, device_id=device(o), device_id_type=MESH)

    lane8 = iota((8, LANES), 1)
    row8 = iota((8, LANES), 0)
    lane16 = iota((CASES, LANES), 1)
    row16 = iota((CASES, LANES), 0)

    for copy in copies[:5]:
        copy.wait()
    gap = jnp.zeros((8, DOFS), F32)
    own_maps = [map_v[s] for s in range(2)]
    for s in range(2):
        high, low = split(jnp.concatenate([own_maps[s], gap], axis=0))
        map_high[32 * (s + 1) : 32 * (s + 2)] = high
        map_low[32 * (s + 1) : 32 * (s + 2)] = low

    coarse = jnp.concatenate([coarse_v[...], jnp.zeros((OWN, LANES - WIN), F32)], axis=1)
    m0, m1, m2 = coarse[0:8], coarse[8:16], coarse[16:24]
    ids = jnp.concatenate([ids_v[...].astype(F32), jnp.zeros((2, LANES - CORNERS), F32)], axis=1)
    id_tile = jnp.full((8, LANES), -1000.0, F32)
    for s in range(2):
        row = jnp.broadcast_to(ids[s : s + 1], (8, LANES))
        for k in range(3):
            id_tile = jnp.where(row8 == 3 * s + k, pltpu.roll(row, 88 - 8 * k, 1), id_tile)
    buf1[slot, 0:8] = jnp.where(lane8 < 64, m0, pltpu.roll(m1, 64, 1))
    second = jnp.where(lane8 < 64, m2, m0)
    second = jnp.where(lane8 >= 72, pltpu.roll(m1, 8, 1), second)
    second = jnp.where(lane8 >= 80, pltpu.roll(m2, 16, 1), second)
    second = jnp.where(lane8 >= 88, id_tile, second)
    buf1[slot, 8:16] = jnp.where(lane8 >= 96, 0.0, second)

    flat = partner_v[...] - (2 * me - 1) * DOFS
    mate_block = flat // LANES
    mate_lane = flat % LANES

    def jumped(extended):
        out = []
        for s in range(2):
            columns = []
            for t in range(4):
                at = slice(t * LANES, (t + 1) * LANES)
                lanes = jnp.broadcast_to(mate_lane[s : s + 1, at], (CASES, LANES))
                block = jnp.broadcast_to(mate_block[s : s + 1, at], (CASES, LANES))
                mate = jnp.zeros((CASES, LANES), F32)
                for b in range(4 * s, 4 * s + 12):
                    source = extended[b // 4][:, b % 4 * LANES : (b % 4 + 1) * LANES]
                    mate = jnp.where(block == b, take_lanes(source, lanes), mate)
                columns.append(extended[s + 1][:, at] - mate)
            out.append(jnp.concatenate(columns, axis=1))
        return out

    def corner_rows(pair):
        tiles = []
        for s in range(2):
            high, low = split(pair[s])
            both = jnp.concatenate([high] * 8 + [low] * 8, axis=0)
            at = slice(32 * (s + 1), 32 * (s + 2))
            maps = jnp.concatenate([map_high[at], map_low[at]], axis=0)
            product = lax.dot_general(
                maps, both, (((1,), (1,)), ((), ())), preferred_element_type=F32
            )
            rows = product[0:32] + product[32:64]
            rows = rows[:, 0:LANES] + rows[:, LANES : 2 * LANES]
            for k in range(3):
                kept = jnp.where(lane8 // 16 == row8, rows[8 * k : 8 * k + 8], 0.0)
                tiles.append(jnp.sum(kept, axis=0, keepdims=True))
        out = jnp.zeros((8, LANES), F32)
        for r in range(6):
            out = jnp.where(row8 == r, tiles[r], out)
        return out

    def products(pair, other):
        total = jnp.zeros((CASES, LANES), F32)
        for s in range(2):
            product = pair[s] * other[s]
            for t in range(4):
                total = total + product[:, t * LANES : (t + 1) * LANES]
        return jnp.sum(total, axis=1, keepdims=True)

    def as_row(column, place):
        kept = jnp.where(lane16 == row16 + 16 * place, column, 0.0)
        return jnp.sum(kept, axis=0, keepdims=True)

    def as_column(row, place):
        spread = jnp.broadcast_to(row, (CASES, LANES))
        kept = jnp.where(lane16 == row16 + 16 * place, spread, 0.0)
        return jnp.sum(kept, axis=1, keepdims=True)

    def times(high, low, v, s):
        top, rest = split(v)
        both = jnp.concatenate([top, rest], axis=0)
        at = slice(DOFS * s, DOFS * s + DOFS)
        product = dot(both, high[at]) + dot(both, low[at])
        return product[0:CASES] + product[CASES : 2 * CASES]

    def cut(source, high, low):
        @pl.loop(0, 16)
        def _(i):
            at = pl.ds(pl.multiple_of(i * 64, 64), 64)
            top, rest = split(source[at])
            high[at] = top
            low[at] = rest

    def halo_copies(n):
        make = functools.partial(pltpu.make_async_remote_copy, device_id_type=MESH)
        return (
            make(src_ref=field.at[n, 1], dst_ref=halo.at[n, 0], send_sem=halo_send.at[n, 0],
                 recv_sem=halo_recv.at[n, 0], device_id=(right,)),
            make(src_ref=field.at[n, 0], dst_ref=halo.at[n, 1], send_sem=halo_send.at[n, 1],
                 recv_sem=halo_recv.at[n, 1], device_id=(left,)),
        )

    def send_halo(n, pair):
        field[n, 0] = pair[0]
        field[n, 1] = pair[1]
        for copy in halo_copies(n):
            copy.start()

    def extended(n):
        for copy in halo_copies(n):
            copy.wait()
        return [halo[n, 0], field[n, 0], field[n, 1], halo[n, 1]]

    def to_all(buf, rows, n, offsets):
        for o in offsets:
            pltpu.make_async_remote_copy(
                src_ref=buf.at[slot, pl.ds(0, rows)], dst_ref=buf.at[slot, pl.ds(0, rows)],
                send_sem=all_send.at[n], recv_sem=all_recv.at[n],
                device_id=device(o), device_id_type=MESH,
            ).start()

    load = [load_v[:, s, :] for s in range(2)]
    buf1[slot, 16:24] = corner_rows(load)

    copies[5].wait()
    cut(inverse_v, inv_high, inv_low)
    solved_load = [times(inv_high, inv_low, load[s], s) for s in range(2)]

    pl.semaphore_wait(barrier, 127)
    same_core = [o for o in OFFSETS if o[3] == 0]
    to_all(buf1, 22, 0, same_core)
    map_copies = (
        pltpu.make_async_remote_copy(
            src_ref=map_v.at[1], dst_ref=map_side.at[0], send_sem=halo_send.at[5, 0],
            recv_sem=halo_recv.at[5, 0], device_id=(right,), device_id_type=MESH),
        pltpu.make_async_remote_copy(
            src_ref=map_v.at[0], dst_ref=map_side.at[1], send_sem=halo_send.at[5, 1],
            recv_sem=halo_recv.at[5, 1], device_id=(left,), device_id_type=MESH),
    )
    for copy in map_copies:
        copy.start()
    send_halo(0, solved_load)
    copies[6].wait()
    cut(schur_v, sch_high, sch_low)
    for s, copy in enumerate(map_copies):
        copy.wait()
        high, low = split(jnp.concatenate([map_side[s], gap], axis=0))
        map_high[96 * s : 96 * s + 32] = high
        map_low[96 * s : 96 * s + 32] = low

    await_bytes(buf1.at[pl.ds(0, 63), pl.ds(0, 22)], all_recv.at[0])
    forward = pltpu.make_async_remote_copy(
        src_ref=buf1.at[pl.ds(core * 64, 64), pl.ds(0, 22)],
        dst_ref=buf1.at[pl.ds(core * 64, 64), pl.ds(0, 22)],
        send_sem=fwd_sem.at[0], recv_sem=fwd_sem.at[1],
        device_id=(zs[0] + xs[0] + ys[0] + cs[1],), device_id_type=MESH,
    )
    forward.start()
    await_bytes(buf1.at[pl.ds(0, 63), pl.ds(0, 22)], all_send.at[0])
    forward.wait()

    packed = buf1[:, 0:16, :].reshape(2048, LANES)
    id_lanes = jnp.transpose(buf1[:, 8:16, :].reshape(1024, LANES))[88:96]
    id_rows[...] = id_lanes.astype(I32)
    lane1024 = iota((8, 1024), 1)
    columns = []
    for dev, rows in ((left, (3, 4, 5)), (me, (0, 1, 2, 3, 4, 5)), (right, (0, 1, 2))):
        for r in rows:
            kept = jnp.where(lane1024 == slot_of(dev) * 8 + r, id_lanes, 0.0)
            columns.append(jnp.sum(kept, axis=1, keepdims=True))
    corner = jnp.concatenate(columns, axis=0).astype(I32)
    owner = corner // OWN
    inner = corner - owner * OWN
    third = inner // 8
    first_row = (owner % 2 * 64 + owner // 2) * 16
    row_a = first_row + inner % 8 + jnp.where(third == 2, 8, 0)
    row_t = first_row + 8 + inner % 8
    wanted = jnp.concatenate([row_a, row_t], axis=0)
    pick = jnp.where(iota((192, 2048), 1) == wanted, 1.0, 0.0).astype(BF16)
    high, low = split(packed)
    found = dot(pick, jnp.concatenate([high, low], axis=1))
    found = found[:, 0:LANES] + found[:, LANES : 2 * LANES]
    lane96 = iota((96, LANES), 1)
    from_a = take_lanes(found[0:96], jnp.minimum(lane96 + jnp.where(third == 1, 64, 0), LANES - 1))
    from_t = take_lanes(found[96:192], jnp.minimum(lane96 + 8 * third, LANES - 1))
    table[:, 0:LANES] = jnp.where(lane96 < 64, from_a, from_t)
    table[:, LANES : 2 * LANES] = jnp.broadcast_to((owner - 1) * OWN, (96, LANES)).astype(F32)

    @pl.loop(0, 48)
    def _(i):
        e, k = i // 6, i % 6
        at = pl.ds(pl.multiple_of(k * 16, 16), 16)
        rows = table[at, 0:LANES]
        base = table[at, LANES : 2 * LANES].astype(I32)
        everyone = id_rows[pl.ds(e, 1), :]
        out = pl.ds(pl.multiple_of(e * 96 + k * 16, 16), 16)
        for b in range(8):
            here = slice(b * LANES, (b + 1) * LANES)
            place = jnp.broadcast_to(everyone[:, here], (16, LANES)) - base
            inside = (place >= 0) & (place < WIN)
            entry = take_lanes(rows, jnp.where(inside, place, 0))
            top, rest = split(jnp.where(inside, entry, 0.0))
            g_high[out, here] = top
            g_low[out, here] = rest

    def spread(buf, first):
        rows = buf[:, first : first + 8, :]
        rows = jnp.where(iota((128, 8, LANES), 1) < 6, rows, 0.0).reshape(1024, LANES)
        top, rest = split(rows)
        both = jnp.concatenate([top, rest], axis=1)
        solved = jnp.zeros((96, 2 * LANES), F32)
        lanes = iota((96, 2 * LANES), 1) % LANES // 16
        for e in range(8):
            at = slice(96 * e, 96 * e + 96)
            part = dot(g_high[at], both) + dot(g_low[at], both)
            solved = jnp.where(lanes == e, part, solved)
        solved = solved[:, 0:LANES] + solved[:, LANES : 2 * LANES]
        for shift in (64, 32, 16):
            solved = solved + pltpu.roll(solved, shift, 1)
        zero = jnp.zeros((8, LANES), F32)
        padded = []
        for j in range(4):
            padded += [solved[24 * j : 24 * j + 24], zero]
        by_case = jnp.transpose(jnp.concatenate(padded, axis=0))[0:CASES]
        stack = []
        for j in range(4):
            stack += list(split(jnp.where(lane16 // 32 == j, by_case, 0.0)))
        stack = jnp.concatenate(stack, axis=0)
        product = dot(stack, map_high[...]) + dot(stack, map_low[...])
        return [product[32 * j : 32 * j + 16] + product[32 * j + 16 : 32 * j + 32] for j in range(4)]

    def add(first, second):
        return [a + b for a, b in zip(first, second)]

    def precondition(n, pair):
        send_halo(n, [times(sch_high, sch_low, pair[s], s) for s in range(2)])
        return [0.5 * v for v in jumped(extended(n))]

    r0 = jumped(add(spread(buf1, 16), extended(0)))
    a = precondition(1, r0)

    buf2[slot] = jnp.where(row8 == 6, as_row(products(r0, a), 0), corner_rows(a))
    to_all(buf2, 7, 1, OFFSETS)
    send_halo(2, [times(inv_high, inv_low, a[s], s) for s in range(2)])
    solved_a = extended(2)
    await_bytes(buf2.at[pl.ds(0, 127), pl.ds(0, 7)], all_recv.at[1])

    q = [2.0 * v for v in jumped(add(spread(buf2, 0), solved_a))]
    current = as_column(jnp.sum(buf2[:, 6, :], axis=0, keepdims=True), 0)
    w = precondition(3, q)

    buf3[slot] = jnp.where(row8 == 6, as_row(products(a, q), 0), corner_rows(w))
    to_all(buf3, 7, 2, OFFSETS)
    send_halo(4, [times(inv_high, inv_low, w[s], s) for s in range(2)])
    solved_w = extended(4)
    await_bytes(buf3.at[pl.ds(0, 127), pl.ds(0, 7)], all_recv.at[2])

    u = [2.0 * v for v in jumped(add(spread(buf3, 0), solved_w))]
    curvature = as_column(jnp.sum(buf3[:, 6, :], axis=0, keepdims=True), 0)
    step0 = current / curvature
    r1 = [r0[s] - step0 * q[s] for s in range(2)]
    z1 = [a[s] - step0 * w[s] for s in range(2)]
    image = [q[s] - step0 * u[s] for s in range(2)]
    cross = products(z1, q) + products(a, image)
    dots = as_row(products(r1, z1), 0) + as_row(products(z1, image), 1) + as_row(cross, 2)
    buf4[slot] = jnp.where(row8 == 0, dots, 0.0)
    to_all(buf4, 1, 3, OFFSETS)
    await_bytes(buf4.at[pl.ds(0, 127), pl.ds(0, 1)], all_recv.at[3])
    total = jnp.sum(buf4[:, 0, :], axis=0, keepdims=True)
    following = as_column(total, 0)
    ratio = following / current
    curvature1 = as_column(total, 1) + ratio * as_column(total, 2) + ratio * ratio * curvature
    step1 = following / curvature1
    for s in range(2):
        mult_ref[:, s, :] = step0 * a[s] + step1 * (z1[s] + ratio * a[s])
        resid_ref[:, s, :] = r1[s] - step1 * (image[s] + ratio * q[s])

    await_bytes(buf2.at[pl.ds(0, 127), pl.ds(0, 7)], all_send.at[1])
    await_bytes(buf3.at[pl.ds(0, 127), pl.ds(0, 7)], all_send.at[2])
    await_bytes(buf4.at[pl.ds(0, 127), pl.ds(0, 1)], all_send.at[3])


def per_device(load, schur_inverse, schur, corner_map, corner_ids, coarse_inverse, partner):
    vmem = pltpu.VMEM
    dma = pltpu.SemaphoreType.DMA
    matrices = (1024, DOFS)
    out = jax.ShapeDtypeStruct(load.shape, F32)

    return pl.pallas_call(
        kernel,
        out_shape=(out, out),
        in_specs=[pl.BlockSpec(memory_space=pl.ANY)] * 7,
        out_specs=(pl.BlockSpec(memory_space=vmem),) * 2,
        scratch_shapes=[
            vmem(load.shape, F32), vmem(matrices, F32), vmem(matrices, F32),
            vmem(corner_map.shape, F32), vmem(corner_ids.shape, I32),
            vmem(coarse_inverse.shape, F32), vmem(partner.shape, I32),
            vmem(matrices, BF16), vmem(matrices, BF16), vmem(matrices, BF16), vmem(matrices, BF16),
            vmem((128, DOFS), BF16), vmem((128, DOFS), BF16), vmem((2, CORNERS, DOFS), F32),
            vmem((96, 2 * LANES), F32), vmem((8, 1024), I32),
            vmem((768, 1024), BF16), vmem((768, 1024), BF16),
            vmem((5, 2, CASES, DOFS), F32), vmem((5, 2, CASES, DOFS), F32),
            vmem((128, 24, LANES), F32), vmem((128, 8, LANES), F32),
            vmem((128, 8, LANES), F32), vmem((128, 8, LANES), F32),
            dma((7,)), dma((4,)), dma((4,)), dma((2,)), dma((6, 2)), dma((6, 2)),
        ],
        compiler_params=pltpu.CompilerParams(
            collective_id=0, has_side_effects=True, vmem_limit_bytes=48 << 20
        ),
    )(
        load, schur_inverse.reshape(matrices), schur.reshape(matrices), corner_map, corner_ids,
        coarse_inverse, partner,
    )


def solution(mesh):
    in_specs = (
        P(None, "sub", None),
        P("sub", None, None),
        P("sub", None, None),
        P("sub", None, None),
        P("sub", None),
        P("sub", None),
        P("sub", None),
    )
    out_specs = (P(None, "sub", None), P(None, "sub", None))
    return jax.shard_map(
        per_device, mesh=mesh, in_specs=in_specs, out_specs=out_specs, check_vma=False
    )
```

time: 1180 us -> 80.4 us (0.07)
  waiting for transfers between devices: 673 us -> 0 us
  blocking collectives: 330 us -> 0 us
  Pallas kernels: 0 us -> 71.1 us
  starting transfers between devices: 62.7 us -> 0 us
  local copies, waits for them, and re-layouts: 59.8 us -> 8.24 us
  other arithmetic: 22.8 us -> 0 us
  between operations: 14.5 us -> 0.66 us
  matrix products: 13.2 us -> 0 us
    unnamed x6 -> x0, waiting for transfers between devices: 643 us -> none
    psum x3 -> x0, blocking collectives: 211 us -> none  [the longest x2 142 us: residual_total(): return lax.psum(products(residual, smoothed), 'sub')]
    all_gather x3 -> x0, blocking collectives: 119 us -> none  [coarse_solve(): solved = lax.all_gather(solved_own, 'sub', axis=1, tiled=True)]
    pallas_call x0 -> x1, Pallas kernels: none -> 71.1 us  [per_device(): pl.pallas_call(kernel, out_shape=(out, out), in_specs=[pl.BlockSpec(memor...]
    ppermute x24 -> x0, starting transfers between devices: 62.6 us -> none  [the longest x12 33 us: with_halo(): after = lax.ppermute(initial, axis, down)]
    gather x12 -> x0, local copies, waits for them, and re-layouts: 41.9 us -> none  [the longest x9 36 us: jumped(): return field - jnp.take(flattened, local_mate, axis=1).reshape(field.shape)]
    ppermute x24 -> x0, waiting for transfers between devices: 30.6 us -> none  [the longest x12 29 us: with_halo(): after = lax.ppermute(initial, axis, down)]
    dot_general x14 -> x0, matrix products: 13.2 us -> none  [the longest x5 9.46 us: blockwise(): jnp.einsum('lsm,smn->lsn', field, matrices, precision=exact_precision)]
  transfers between devices with their start and end apart: 27 -> 0, of which waited for: 14 -> 0; matrix products, arithmetic and copies ran while one was open for 0% -> 0% of each run, Pallas kernels for 0% -> 0%
where the time goes in v1:
time: 80.4 us; the launch traced here: 80 us
  Pallas kernels  71.1 us (88%)
  local copies, waits for them, and re-layouts  8.24 us (10%)
    pallas_call x1, Pallas kernels, per_device(): pl.pallas_call(kernel, out_shape=(out, out), in_specs=[pl.BlockSpec(memor...  71.1 us
    unnamed x16, local copies, waits for them, and re-layouts  8.24 us

profile of v1, /device:TPU:1, one launch (start us, length us, event | category | flops | bytes accessed | tf_op | source)
XLA Modules:
  0.0 80.0 jit_solution(11637961642098465893)
XLA Ops:
  0.6 0.0 copy-start
  0.6 1.6 %copy-done = f32[2,512,512]{2,1,0:T(8,128)S(1)} copy-done((f32[2,512,512]{2,1,0:T(8,128)S(1)}, f32[2,512,512]{2,1,0:T(8,128)}, u32[]{:S(2)}) %copy-start) | copy-done | bytes 2097176
  2.2 0.0 copy-start.1
  2.2 1.6 %copy-done.1 = f32[2,512,512]{2,1,0:T(8,128)S(1)} copy-done((f32[2,512,512]{2,1,0:T(8,128)S(1)}, f32[2,512,512]{2,1,0:T(8,128)}, u32[]{:S(2)}) %copy-start.1) | copy-done | bytes 2097176
  3.8 0.0 copy-start.2
  3.8 0.9 %copy-done.2 = f32[2,24,512]{2,1,0:T(8,128)S(1)} copy-done((f32[2,24,512]{2,1,0:T(8,128)S(1)}, f32[2,24,512]{2,1,0:T(8,128)}, u32[]{:S(2)}) %copy-start.2) | copy-done | bytes 98328
  4.7 0.0 copy-start.3
  4.7 0.8 %copy-done.3 = f32[16,2,512]{2,1,0:T(2,128)S(1)} copy-done((f32[16,2,512]{2,1,0:T(2,128)S(1)}, f32[16,2,512]{2,1,0:T(2,128)}, u32[]{:S(2)}) %copy-start.3) | copy-done | bytes 65560
  5.5 0.0 copy-start.4
  5.6 0.7 copy-done.4
  6.3 0.0 copy-start.5
  6.3 0.7 copy-done.5
  6.9 0.0 copy-start.6
  6.9 0.7 copy-done.6
  7.6 71.1 %shard_map.86 = (f32[16,2,512]{2,1,0:T(2,128)S(1)}, f32[16,2,512]{2,1,0:T(2,128)S(1)}) custom-call(f32[16,2,512]{2,1,0:T(2,128)S(1)} %copy-done.3, f32[1024,512]{1,0:T(8,128)S(1)} %bitcast.2, f32[1024,512]{1,0:T(8,128)S(1)} %bitcast.3, f32[2,24,512]{2,1,0:T(8,128)S(1)} %copy-done.2, s32[2,24]{1,0:T(2,128)S(1)} %copy-done.6, f32[24,72]{1,0:T(8,128)S(1)} %copy-done.4, ...), custom_call_target="tpu_custom_call" | custom-call | tf_op jit(solution)/shard_map/pallas_call | solution.py:377
  78.8 0.6 copy.11
  79.4 0.6 copy.12
Async XLA Ops:
  0.6 1.6 %copy-start = (f32[2,512,512]{2,1,0:T(8,128)S(1)}, f32[2,512,512]{2,1,0:T(8,128)}, u32[]{:S(2)}) copy-start(f32[2,512,512]{2,1,0:T(8,128)} %param.8) | copy-start | bytes 6291460
  2.2 1.6 %copy-start.1 = (f32[2,512,512]{2,1,0:T(8,128)S(1)}, f32[2,512,512]{2,1,0:T(8,128)}, u32[]{:S(2)}) copy-start(f32[2,512,512]{2,1,0:T(8,128)} %param.9) | copy-start | bytes 6291460
  3.8 0.9 %copy-start.2 = (f32[2,24,512]{2,1,0:T(8,128)S(1)}, f32[2,24,512]{2,1,0:T(8,128)}, u32[]{:S(2)}) copy-start(f32[2,24,512]{2,1,0:T(8,128)} %map_hbm.1) | copy-start | bytes 294916
  4.7 0.8 %copy-start.3 = (f32[16,2,512]{2,1,0:T(2,128)S(1)}, f32[16,2,512]{2,1,0:T(2,128)}, u32[]{:S(2)}) copy-start(f32[16,2,512]{2,1,0:T(2,128)} %load_hbm.1) | copy-start | bytes 196612
  5.5 0.7 copy-start.4
  6.3 0.7 copy-start.5
  6.9 0.7 copy-start.6

commit v2 on v1

v2 whole, which is shorter than its diff:
```python
import functools
import itertools

import jax
import jax.numpy as jnp
from jax import lax
from jax.experimental import pallas as pl
from jax.experimental.pallas import tpu as pltpu
from jax.sharding import PartitionSpec as P

MESH = pl.DeviceIdType.MESH
F32, BF16, I32 = jnp.float32, jnp.bfloat16, jnp.int32
CASES, DOFS, CORNERS, OWN, WIN = 16, 512, 24, 24, 72
LANES = 128
HOPS = (0, 1, 2, 1)

CHIPS = sorted(
    itertools.product(range(4), repeat=3), key=lambda o: HOPS[o[0]] + HOPS[o[1]] + HOPS[o[2]]
)
NEAR = 57


def hops(i):
    return sum(HOPS[d] for d in CHIPS[i])


FAR_SENDS = [(64 * c + i, CHIPS[i], c) for i in range(NEAR, 64) for c in range(2)]
NEAR_SENDS = [(i, CHIPS[i], 0) for i in range(1, NEAR)]
SENDS = sorted(
    FAR_SENDS + NEAR_SENDS, key=lambda t: -(hops(t[0] % 64) + (2 if t[0] < NEAR else 0))
)
EVERYONE = sorted(
    [(64 * c + i, CHIPS[i], c) for i in range(64) for c in range(2) if i + c > 0],
    key=lambda t: -hops(t[0] % 64),
)


def split(v):
    high = v.astype(BF16)
    return high, (v - high.astype(F32)).astype(BF16)


def await_bytes(ref, sem):
    pltpu.make_async_copy(ref, ref, sem).wait()


def dot(a, b):
    return jnp.dot(a, b, preferred_element_type=F32)


def take_lanes(values, lanes):
    return jnp.take_along_axis(values, lanes, axis=1, mode="promise_in_bounds")


def iota(shape, dim):
    return lax.broadcasted_iota(I32, shape, dim)


def kernel(
    load_hbm, inverse_hbm, schur_hbm, map_hbm, ids_hbm, coarse_hbm, partner_hbm,
    mult_ref, resid_ref,
    load_v, inverse_v, schur_v, map_v, ids_v, coarse_v, partner_v,
    inverse_parts, schur_parts, map_high, map_low, map_side, id_side,
    table, bases, id_rows, operator, field, halo, coarse_buf, buf1, buf2, buf3, buf4,
    in_sem, all_send, near_recv, far_recv, fwd_send, fwd_recv, halo_send, halo_recv,
):
    me = lax.axis_index("sub")
    core, chip = me % 2, me // 2
    y, x, z = chip % 4, chip // 4 % 4, chip // 16
    zs = [(z + i) % 4 * 32 for i in range(4)]
    xs = [(x + i) % 4 * 8 for i in range(4)]
    ys = [(y + i) % 4 * 2 for i in range(4)]
    cs = [core, 1 - core]
    right, left = (me + 1) % 128, (me + 127) % 128

    def device(o, c):
        return (zs[o[0]] + xs[o[1]] + ys[o[2]] + cs[c],)

    pairs = (
        (map_hbm, map_v), (load_hbm, load_v), (ids_hbm, ids_v), (coarse_hbm, coarse_v),
        (partner_hbm, partner_v), (inverse_hbm, inverse_v), (schur_hbm, schur_v),
    )
    copies = [pltpu.make_async_copy(a, b, in_sem.at[i]) for i, (a, b) in enumerate(pairs)]
    for copy in copies:
        copy.start()

    barrier = pltpu.get_barrier_semaphore()
    for _, o, c in EVERYONE:
        pl.semaphore_signal(barrier, inc=1, device_id=device(o, c), device_id_type=MESH)

    lane8 = iota((8, LANES), 1)
    row8 = iota((8, LANES), 0)
    lane16 = iota((CASES, LANES), 1)
    row16 = iota((CASES, LANES), 0)

    for copy in copies[:5]:
        copy.wait()
    gap = jnp.zeros((8, DOFS), F32)
    own_maps = [map_v[s] for s in range(2)]
    for s in range(2):
        high, low = split(jnp.concatenate([own_maps[s], gap], axis=0))
        map_high[32 * (s + 1) : 32 * (s + 2)] = high
        map_low[32 * (s + 1) : 32 * (s + 2)] = low

    coarse = jnp.concatenate([coarse_v[...], jnp.zeros((OWN, LANES - WIN), F32)], axis=1)
    m0, m1, m2 = coarse[0:8], coarse[8:16], coarse[16:24]
    ids = jnp.concatenate([ids_v[...].astype(F32), jnp.zeros((2, LANES - CORNERS), F32)], axis=1)
    ids = jnp.where(lane8[0:1] < CORNERS, ids[0:1], pltpu.roll(ids, CORNERS, 1)[1:2])
    ids = jnp.where(lane8[0:1] < 2 * CORNERS, ids, me.astype(F32))
    coarse_buf[0, 0:8] = jnp.where(lane8 < 64, m0, pltpu.roll(m1, 64, 1))
    second = jnp.where(lane8 < 64, m2, m0)
    second = jnp.where(lane8 >= 72, pltpu.roll(m1, 8, 1), second)
    second = jnp.where(lane8 >= 80, pltpu.roll(m2, 16, 1), second)
    coarse_buf[0, 8:16] = jnp.where(lane8 >= 88, 0.0, second)
    coarse_buf[0, 16:17] = ids

    flat = partner_v[...] - (2 * me - 1) * DOFS
    mate_block = flat // LANES
    mate_lane = flat % LANES

    def jumped(extended):
        out = []
        for s in range(2):
            columns = []
            for t in range(4):
                at = slice(t * LANES, (t + 1) * LANES)
                lanes = jnp.broadcast_to(mate_lane[s : s + 1, at], (CASES, LANES))
                block = jnp.broadcast_to(mate_block[s : s + 1, at], (CASES, LANES))
                mate = jnp.zeros((CASES, LANES), F32)
                for b in range(4 * s, 4 * s + 12):
                    source = extended[b // 4][:, b % 4 * LANES : (b % 4 + 1) * LANES]
                    mate = jnp.where(block == b, take_lanes(source, lanes), mate)
                columns.append(extended[s + 1][:, at] - mate)
            out.append(jnp.concatenate(columns, axis=1))
        return out

    def corner_rows(pair):
        tiles = []
        for s in range(2):
            high, low = split(pair[s])
            both = jnp.concatenate([high] * 8 + [low] * 8, axis=0)
            at = slice(32 * (s + 1), 32 * (s + 2))
            maps = jnp.concatenate([map_high[at], map_low[at]], axis=0)
            product = lax.dot_general(
                maps, both, (((1,), (1,)), ((), ())), preferred_element_type=F32
            )
            rows = product[0:32] + product[32:64]
            rows = rows[:, 0:LANES] + rows[:, LANES : 2 * LANES]
            for k in range(3):
                kept = jnp.where(lane8 // 16 == row8, rows[8 * k : 8 * k + 8], 0.0)
                tiles.append(jnp.sum(kept, axis=0, keepdims=True))
        out = jnp.zeros((8, LANES), F32)
        for r in range(6):
            out = jnp.where(row8 == r, tiles[r], out)
        return out

    def products(pair, other):
        total = jnp.zeros((CASES, LANES), F32)
        for s in range(2):
            product = pair[s] * other[s]
            for t in range(4):
                total = total + product[:, t * LANES : (t + 1) * LANES]
        return jnp.sum(total, axis=1, keepdims=True)

    def as_row(column, place):
        kept = jnp.where(lane16 == row16 + 16 * place, column, 0.0)
        return jnp.sum(kept, axis=0, keepdims=True)

    def as_column(row, place):
        spread = jnp.broadcast_to(row, (CASES, LANES))
        kept = jnp.where(lane16 == row16 + 16 * place, spread, 0.0)
        return jnp.sum(kept, axis=1, keepdims=True)

    def times(parts, v, s):
        top, rest = split(v)
        both = jnp.concatenate([top, rest], axis=0)
        product = dot(jnp.concatenate([both, both], axis=1), parts[s])
        return product[0:CASES] + product[CASES : 2 * CASES]

    def cut(source, parts):
        for s in range(2):

            @pl.loop(0, 8)
            def _(i):
                at = pl.multiple_of(i * 64, 64)
                top, rest = split(source[s, pl.ds(at, 64)])
                parts[s, pl.ds(at, 64)] = top
                parts[s, pl.ds(at + DOFS, 64)] = rest

    def halo_copies(n):
        make = functools.partial(pltpu.make_async_remote_copy, device_id_type=MESH)
        return (
            make(src_ref=field.at[n, 1], dst_ref=halo.at[n, 0], send_sem=halo_send.at[n, 0],
                 recv_sem=halo_recv.at[n, 0], device_id=(right,)),
            make(src_ref=field.at[n, 0], dst_ref=halo.at[n, 1], send_sem=halo_send.at[n, 1],
                 recv_sem=halo_recv.at[n, 1], device_id=(left,)),
        )

    def send_halo(n, pair):
        field[n, 0] = pair[0]
        field[n, 1] = pair[1]
        for copy in halo_copies(n):
            copy.start()

    def extended(n):
        for copy in halo_copies(n):
            copy.wait()
        return [halo[n, 0], field[n, 0], field[n, 1], halo[n, 1]]

    def to_all(buf, rows, n):
        part = pl.ds(0, rows)
        for to, o, c in SENDS:
            pltpu.make_async_remote_copy(
                src_ref=buf.at[0, part], dst_ref=buf.at[to, part], send_sem=all_send.at[n],
                recv_sem=(near_recv if to < NEAR else far_recv).at[n],
                device_id=device(o, c), device_id_type=MESH,
            ).start()

    def forward(buf, rows, n):
        return pltpu.make_async_remote_copy(
            src_ref=buf.at[pl.ds(0, NEAR), pl.ds(0, rows)],
            dst_ref=buf.at[pl.ds(64, NEAR), pl.ds(0, rows)],
            send_sem=fwd_send.at[n], recv_sem=fwd_recv.at[n],
            device_id=device((0, 0, 0), 1), device_id_type=MESH,
        )

    def pass_on(buf, rows, n):
        await_bytes(buf.at[pl.ds(0, len(NEAR_SENDS)), pl.ds(0, rows)], near_recv.at[n])
        forward(buf, rows, n).start()

    def from_all(buf, rows, n):
        await_bytes(buf.at[pl.ds(0, len(FAR_SENDS)), pl.ds(0, rows)], far_recv.at[n])
        await_bytes(buf.at[pl.ds(0, len(SENDS)), pl.ds(0, rows)], all_send.at[n])
        forward(buf, rows, n).wait()

    load = [load_v[:, s, :] for s in range(2)]
    buf1[0] = corner_rows(load)
    copies[5].wait()
    cut(inverse_v, inverse_parts)
    solved_load = [times(inverse_parts, load[s], s) for s in range(2)]

    pl.semaphore_wait(barrier, 127)
    to_all(coarse_buf, 17, 0)
    to_all(buf1, 6, 1)
    side_copies = []
    for i, (dev, near) in enumerate(((right, 1), (left, 0))):
        for n, (src, dst) in enumerate(
            ((map_v.at[near], map_side.at[i]), (coarse_buf.at[0, pl.ds(16, 1)], id_side.at[i]))
        ):
            side_copies.append(
                pltpu.make_async_remote_copy(
                    src_ref=src, dst_ref=dst, send_sem=halo_send.at[5 + n, i],
                    recv_sem=halo_recv.at[5 + n, i], device_id=(dev,), device_id_type=MESH,
                )
            )
    for copy in side_copies:
        copy.start()
    send_halo(0, solved_load)
    copies[6].wait()
    cut(schur_v, schur_parts)
    for copy in side_copies:
        copy.wait()
    for i in range(2):
        high, low = split(jnp.concatenate([map_side[i], gap], axis=0))
        map_high[96 * i : 96 * i + 32] = high
        map_low[96 * i : 96 * i + 32] = low
    row48 = iota((48, LANES), 0)
    lane48 = iota((48, LANES), 1)

    def id_column(row):
        kept = jnp.where(row48 == lane48, jnp.broadcast_to(row, (48, LANES)), 0.0)
        return jnp.sum(kept, axis=1, keepdims=True)

    corner = jnp.concatenate(
        [id_column(id_side[0])[24:48], id_column(ids), id_column(id_side[1])[0:24]], axis=0
    ).astype(I32)
    owner = corner // OWN
    inner = corner - owner * OWN
    third = inner // 8
    pass_on(coarse_buf, 17, 0)
    pass_on(buf1, 6, 1)
    from_all(coarse_buf, 17, 0)

    id_lanes = jnp.transpose(coarse_buf[:, 16, :])
    id_rows[...] = id_lanes[0:48].astype(I32)
    owned = jnp.where(id_lanes[48:49].astype(I32) == owner, 1.0, 0.0)
    wanted = jnp.concatenate([inner % 8 + jnp.where(third == 2, 8, 0), 8 + inner % 8], axis=0)
    owned = jnp.concatenate([owned, owned], axis=0)
    pick = jnp.concatenate(
        [jnp.where(wanted == r, owned, 0.0).astype(BF16) for r in range(16)], axis=1
    )
    high, low = split(jnp.concatenate([coarse_buf[:, r, :] for r in range(16)], axis=0))
    found = dot(pick, jnp.concatenate([high, low], axis=1))
    found = found[:, 0:LANES] + found[:, LANES : 2 * LANES]
    lane96 = iota((96, LANES), 1)
    from_a = take_lanes(found[0:96], jnp.minimum(lane96 + jnp.where(third == 1, 64, 0), LANES - 1))
    from_t = take_lanes(found[96:192], jnp.minimum(lane96 + 8 * third, LANES - 1))
    table[...] = jnp.where(lane96 < 64, from_a, jnp.where(lane96 < WIN, from_t, 0.0))
    bases[...] = jnp.broadcast_to((owner - 1) * OWN, (96, LANES))

    @pl.loop(0, 8)
    def _(e):
        everyone = [id_rows[pl.ds(8 * r + e, 1), :] for r in range(6)]
        for k in range(6):
            rows = table[16 * k : 16 * k + 16]
            base = bases[16 * k : 16 * k + 16]
            out = pl.ds(pl.multiple_of(e * 96 + k * 16, 16), 16)
            for r in range(6):
                place = jnp.broadcast_to(everyone[r], (16, LANES)) - base
                place = jnp.where((place < 0) | (place >= WIN), LANES - 1, place)
                top, rest = split(take_lanes(rows, place))
                operator[out, r * LANES : (r + 1) * LANES] = top
                operator[out, (r + 6) * LANES : (r + 7) * LANES] = rest

    from_all(buf1, 6, 1)

    def spread(buf):
        top, rest = split(jnp.concatenate([buf[:, r, :] for r in range(6)], axis=0))
        both = jnp.concatenate([top, rest], axis=1)
        product = dot(operator[...], jnp.concatenate([both, both], axis=0))
        solved = jnp.zeros((96, 2 * LANES), F32)
        lanes = iota((96, 2 * LANES), 1) % LANES // 16
        for e in range(8):
            solved = jnp.where(lanes == e, product[96 * e : 96 * e + 96], solved)
        solved = solved[:, 0:LANES] + solved[:, LANES : 2 * LANES]
        zero = jnp.zeros((8, LANES), F32)
        padded = []
        for j in range(4):
            padded += [solved[24 * j : 24 * j + 24], zero]
        turned = jnp.transpose(jnp.concatenate(padded, axis=0))
        by_case = turned[0:CASES]
        for e in range(1, 8):
            by_case = by_case + turned[CASES * e : CASES * e + CASES]
        stack = []
        for j in range(4):
            stack += list(split(jnp.where(lane16 // 32 == j, by_case, 0.0)))
        stack = jnp.concatenate(stack, axis=0)
        product = dot(stack, map_high[...]) + dot(stack, map_low[...])
        return [product[32 * j : 32 * j + 16] + product[32 * j + 16 : 32 * j + 32] for j in range(4)]

    def add(first, second):
        return [a + b for a, b in zip(first, second)]

    def precondition(n, pair):
        send_halo(n, [times(schur_parts, pair[s], s) for s in range(2)])
        return [0.5 * v for v in jumped(extended(n))]

    r0 = jumped(add(spread(buf1), extended(0)))
    a = precondition(1, r0)

    buf2[0] = corner_rows(a)
    to_all(buf2, 6, 2)
    send_halo(2, [times(inverse_parts, a[s], s) for s in range(2)])
    pass_on(buf2, 6, 2)
    solved_a = extended(2)
    from_all(buf2, 6, 2)

    q = [2.0 * v for v in jumped(add(spread(buf2), solved_a))]
    send_halo(3, [times(schur_parts, q[s], s) for s in range(2)])
    dots = as_row(products(r0, a), 0) + as_row(products(a, q), 1)
    w = [0.5 * v for v in jumped(extended(3))]

    buf3[0] = jnp.where(row8 == 6, dots, corner_rows(w))
    to_all(buf3, 7, 3)
    send_halo(4, [times(inverse_parts, w[s], s) for s in range(2)])
    pass_on(buf3, 7, 3)
    solved_w = extended(4)
    from_all(buf3, 7, 3)

    u = [2.0 * v for v in jumped(add(spread(buf3), solved_w))]
    total = jnp.sum(buf3[:, 6, :], axis=0, keepdims=True)
    current, curvature = as_column(total, 0), as_column(total, 1)
    step0 = current / curvature
    r1 = [r0[s] - step0 * q[s] for s in range(2)]
    z1 = [a[s] - step0 * w[s] for s in range(2)]
    image = [q[s] - step0 * u[s] for s in range(2)]
    cross = products(z1, q) + products(a, image)
    dots = as_row(products(r1, z1), 0) + as_row(products(z1, image), 1) + as_row(cross, 2)
    buf4[0] = jnp.where(row8 == 0, dots, 0.0)
    for to, o, c in EVERYONE:
        pltpu.make_async_remote_copy(
            src_ref=buf4.at[0, pl.ds(0, 1)], dst_ref=buf4.at[to, pl.ds(0, 1)],
            send_sem=all_send.at[4], recv_sem=far_recv.at[4],
            device_id=device(o, c), device_id_type=MESH,
        ).start()
    await_bytes(buf4.at[pl.ds(0, 127), pl.ds(0, 1)], far_recv.at[4])
    total = jnp.sum(buf4[:, 0, :], axis=0, keepdims=True)
    following = as_column(total, 0)
    ratio = following / current
    curvature1 = as_column(total, 1) + ratio * as_column(total, 2) + ratio * ratio * curvature
    step1 = following / curvature1
    for s in range(2):
        mult_ref[:, s, :] = step0 * a[s] + step1 * (z1[s] + ratio * a[s])
        resid_ref[:, s, :] = r1[s] - step1 * (image[s] + ratio * q[s])

    await_bytes(buf4.at[pl.ds(0, 127), pl.ds(0, 1)], all_send.at[4])


def per_device(load, schur_inverse, schur, corner_map, corner_ids, coarse_inverse, partner):
    vmem = pltpu.VMEM
    dma = pltpu.SemaphoreType.DMA
    out = jax.ShapeDtypeStruct(load.shape, F32)
    inputs = (load, schur_inverse, schur, corner_map, corner_ids, coarse_inverse, partner)
    parts = vmem((2, 2 * DOFS, DOFS), BF16)
    slots = vmem((128, 8, LANES), F32)
    return pl.pallas_call(
        kernel,
        out_shape=(out, out),
        in_specs=[pl.BlockSpec(memory_space=pltpu.HBM)] * 7,
        out_specs=(pl.BlockSpec(memory_space=vmem),) * 2,
        scratch_shapes=[
            *(vmem(v.shape, v.dtype) for v in inputs),
            parts, parts,
            vmem((128, DOFS), BF16), vmem((128, DOFS), BF16),
            vmem((2, CORNERS, DOFS), F32), vmem((2, 1, LANES), F32),
            vmem((96, LANES), F32), vmem((96, LANES), I32), vmem((48, LANES), I32),
            vmem((768, 1536), BF16),
            vmem((5, 2, CASES, DOFS), F32), vmem((5, 2, CASES, DOFS), F32),
            vmem((128, 24, LANES), F32), slots, slots, slots, slots,
            dma((7,)), dma((5,)), dma((5,)), dma((5,)), dma((4,)), dma((4,)),
            dma((7, 2)), dma((7, 2)),
        ],
        compiler_params=pltpu.CompilerParams(
            collective_id=0, has_side_effects=True, vmem_limit_bytes=63 << 20
        ),
    )(*inputs)


def solution(mesh):
    in_specs = (
        P(None, "sub", None),
        P("sub", None, None),
        P("sub", None, None),
        P("sub", None, None),
        P("sub", None),
        P("sub", None),
        P("sub", None),
    )
    out_specs = (P(None, "sub", None), P(None, "sub", None))
    return jax.shard_map(
        per_device, mesh=mesh, in_specs=in_specs, out_specs=out_specs, check_vma=False
    )
```

time: 80.4 us -> 73.6 us (0.915)
  local copies, waits for them, and re-layouts: 8.24 us -> 2.95 us
  Pallas kernels: 71.1 us -> 69.8 us
    unnamed x16 -> x2, local copies, waits for them, and re-layouts: 8.24 us -> 2.95 us
    pallas_call x1, Pallas kernels: 71.1 us -> 69.8 us  [per_device(): pl.pallas_call(kernel, out_shape=(out, out), in_specs=[pl.BlockSpec(memor...]
where the time goes in v2:
time: 73.6 us; the launch traced here: 73.4 us
  Pallas kernels  69.8 us (95%)
  local copies, waits for them, and re-layouts  2.95 us (4%)
    pallas_call x1, Pallas kernels, per_device(): pl.pallas_call(kernel, out_shape=(out, out), in_specs=[pl.BlockSpec(memor...  69.8 us
    unnamed x2, local copies, waits for them, and re-layouts  2.95 us

profile of v2, /device:TPU:1, one launch (start us, length us, event | category | flops | bytes accessed | tf_op | source)
XLA Modules:
  0.0 73.4 jit_solution(8296023992665878605)
XLA Ops:
  0.6 69.8 %shard_map.86 = (f32[16,2,512]{2,1,0:T(2,128)}, f32[16,2,512]{2,1,0:T(2,128)}) custom-call(f32[16,2,512]{2,1,0:T(2,128)} %load_hbm.1, f32[2,512,512]{2,1,0:T(8,128)} %inverse_hbm.1, f32[2,512,512]{2,1,0:T(8,128)} %schur_hbm.1, f32[2,24,512]{2,1,0:T(8,128)} %map_hbm.1, s32[2,24]{1,0:T(2,128)} %ids_hbm.1, f32[24,72]{1,0:T(8,128)} %coarse_hbm.1, ...), custom_call_target="tpu_custom_call" | custom-call | tf_op jit(solution)/shard_map/pallas_call | solution.py:406
  70.4 1.5 %copy.11 = f32[16,2,512]{2,1,0:T(2,128)} copy(f32[16,2,512]{2,1,0:T(2,128)} %get-tuple-element.4) | data formatting | bytes 131072
  71.9 1.5 %copy.12 = f32[16,2,512]{2,1,0:T(2,128)} copy(f32[16,2,512]{2,1,0:T(2,128)} %get-tuple-element.5) | data formatting | bytes 131072

commit v3 on v2

--- a/solution.py
+++ b/solution.py
@@ -15,24 +15,13 @@
 HOPS = (0, 1, 2, 1)
 
 CHIPS = sorted(
-    itertools.product(range(4), repeat=3), key=lambda o: HOPS[o[0]] + HOPS[o[1]] + HOPS[o[2]]
+    itertools.product(range(4), repeat=3), key=lambda o: -sum(HOPS[d] for d in o)
 )
-NEAR = 57
-
-
-def hops(i):
-    return sum(HOPS[d] for d in CHIPS[i])
-
-
-FAR_SENDS = [(64 * c + i, CHIPS[i], c) for i in range(NEAR, 64) for c in range(2)]
-NEAR_SENDS = [(i, CHIPS[i], 0) for i in range(1, NEAR)]
-SENDS = sorted(
-    FAR_SENDS + NEAR_SENDS, key=lambda t: -(hops(t[0] % 64) + (2 if t[0] < NEAR else 0))
-)
-EVERYONE = sorted(
-    [(64 * c + i, CHIPS[i], c) for i in range(64) for c in range(2) if i + c > 0],
-    key=lambda t: -hops(t[0] % 64),
-)
+ROUTES = ((2, 1, 0), (1, 0, 2), (0, 2, 1))
+
+
+def place_of(o):
+    return sum(o[axis] * 4**k for k, axis in enumerate(ROUTES[2]))
 
 
 def split(v):
@@ -61,8 +50,8 @@
     mult_ref, resid_ref,
     load_v, inverse_v, schur_v, map_v, ids_v, coarse_v, partner_v,
     inverse_parts, schur_parts, map_high, map_low, map_side, id_side,
-    table, bases, id_rows, operator, field, halo, coarse_buf, buf1, buf2, buf3, buf4,
-    in_sem, all_send, near_recv, far_recv, fwd_send, fwd_recv, halo_send, halo_recv,
+    table, bases, id_rows, operator, field, halo, coarse_a, coarse_b, buf1, buf2, buf3, buf4,
+    in_sem, stage_send, stage_recv, all_send, all_recv, fwd_send, fwd_recv, halo_send, halo_recv,
 ):
     me = lax.axis_index("sub")
     core, chip = me % 2, me // 2
@@ -76,6 +65,9 @@
     def device(o, c):
         return (zs[o[0]] + xs[o[1]] + ys[o[2]] + cs[c],)
 
+    def steps(axis, k):
+        return tuple(k if i == axis else 0 for i in range(3))
+
     pairs = (
         (map_hbm, map_v), (load_hbm, load_v), (ids_hbm, ids_v), (coarse_hbm, coarse_v),
         (partner_hbm, partner_v), (inverse_hbm, inverse_v), (schur_hbm, schur_v),
@@ -85,8 +77,10 @@
         copy.start()
 
     barrier = pltpu.get_barrier_semaphore()
-    for _, o, c in EVERYONE:
-        pl.semaphore_signal(barrier, inc=1, device_id=device(o, c), device_id_type=MESH)
+    partners = [device(steps(axis, k), 0) for axis in range(3) for k in (2, 1, 3)]
+    partners += [(jnp.where(core == 0, left, right),), device((0, 0, 0), 1)]
+    for partner in partners:
+        pl.semaphore_signal(barrier, inc=1, device_id=partner, device_id_type=MESH)
 
     lane8 = iota((8, LANES), 1)
     row8 = iota((8, LANES), 0)
@@ -106,13 +100,11 @@
     m0, m1, m2 = coarse[0:8], coarse[8:16], coarse[16:24]
     ids = jnp.concatenate([ids_v[...].astype(F32), jnp.zeros((2, LANES - CORNERS), F32)], axis=1)
     ids = jnp.where(lane8[0:1] < CORNERS, ids[0:1], pltpu.roll(ids, CORNERS, 1)[1:2])
-    ids = jnp.where(lane8[0:1] < 2 * CORNERS, ids, me.astype(F32))
-    coarse_buf[0, 0:8] = jnp.where(lane8 < 64, m0, pltpu.roll(m1, 64, 1))
+    coarse_a[0] = jnp.where(lane8 < 64, m0, pltpu.roll(m1, 64, 1))
     second = jnp.where(lane8 < 64, m2, m0)
     second = jnp.where(lane8 >= 72, pltpu.roll(m1, 8, 1), second)
     second = jnp.where(lane8 >= 80, pltpu.roll(m2, 16, 1), second)
-    coarse_buf[0, 8:16] = jnp.where(lane8 >= 88, 0.0, second)
-    coarse_buf[0, 16:17] = ids
+    coarse_b[0] = jnp.where(lane8 >= 88, 0.0, second)
 
     flat = partner_v[...] - (2 * me - 1) * DOFS
     mate_block = flat // LANES
@@ -209,43 +201,53 @@
 
     def to_all(buf, rows, n):
         part = pl.ds(0, rows)
-        for to, o, c in SENDS:
+        for o in CHIPS[:-1]:
             pltpu.make_async_remote_copy(
-                src_ref=buf.at[0, part], dst_ref=buf.at[to, part], send_sem=all_send.at[n],
-                recv_sem=(near_recv if to < NEAR else far_recv).at[n],
-                device_id=device(o, c), device_id_type=MESH,
+                src_ref=buf.at[0, part], dst_ref=buf.at[place_of(o), part],
+                send_sem=all_send.at[n], recv_sem=all_recv.at[n],
+                device_id=device(o, 0), device_id_type=MESH,
             ).start()
 
     def forward(buf, rows, n):
         return pltpu.make_async_remote_copy(
-            src_ref=buf.at[pl.ds(0, NEAR), pl.ds(0, rows)],
-            dst_ref=buf.at[pl.ds(64, NEAR), pl.ds(0, rows)],
+            src_ref=buf.at[pl.ds(0, 64), pl.ds(0, rows)],
+            dst_ref=buf.at[pl.ds(64, 64), pl.ds(0, rows)],
             send_sem=fwd_send.at[n], recv_sem=fwd_recv.at[n],
             device_id=device((0, 0, 0), 1), device_id_type=MESH,
         )
 
-    def pass_on(buf, rows, n):
-        await_bytes(buf.at[pl.ds(0, len(NEAR_SENDS)), pl.ds(0, rows)], near_recv.at[n])
-        forward(buf, rows, n).start()
-
     def from_all(buf, rows, n):
-        await_bytes(buf.at[pl.ds(0, len(FAR_SENDS)), pl.ds(0, rows)], far_recv.at[n])
-        await_bytes(buf.at[pl.ds(0, len(SENDS)), pl.ds(0, rows)], all_send.at[n])
-        forward(buf, rows, n).wait()
+        others = buf.at[pl.ds(0, 63), pl.ds(0, rows)]
+        await_bytes(others, all_recv.at[n])
+        copy = forward(buf, rows, n)
+        copy.start()
+        await_bytes(others, all_send.at[n])
+        copy.wait()
+
+    thirds = (coarse_a, coarse_b, buf1)
+
+    def send_stage(third, stage):
+        buf, axis, size = thirds[third], ROUTES[third][stage], 4**stage
+        for k in (2, 1, 3):
+            pltpu.make_async_remote_copy(
+                src_ref=buf.at[pl.ds(0, size)], dst_ref=buf.at[pl.ds(k * size, size)],
+                send_sem=stage_send.at[third, stage], recv_sem=stage_recv.at[third, stage],
+                device_id=device(steps(axis, k), 0), device_id_type=MESH,
+            ).start()
+
+    def await_stage(sems, third, stage):
+        await_bytes(thirds[third].at[pl.ds(0, 3 * 4**stage)], sems.at[third, stage])
 
     load = [load_v[:, s, :] for s in range(2)]
-    buf1[0] = corner_rows(load)
-    copies[5].wait()
-    cut(inverse_v, inverse_parts)
-    solved_load = [times(inverse_parts, load[s], s) for s in range(2)]
-
-    pl.semaphore_wait(barrier, 127)
-    to_all(coarse_buf, 17, 0)
-    to_all(buf1, 6, 1)
+    buf1[0] = jnp.where(row8 == 6, ids, corner_rows(load))
+
+    pl.semaphore_wait(barrier, len(partners))
+    for third in range(3):
+        send_stage(third, 0)
     side_copies = []
     for i, (dev, near) in enumerate(((right, 1), (left, 0))):
         for n, (src, dst) in enumerate(
-            ((map_v.at[near], map_side.at[i]), (coarse_buf.at[0, pl.ds(16, 1)], id_side.at[i]))
+            ((map_v.at[near], map_side.at[i]), (buf1.at[0, pl.ds(6, 1)], id_side.at[i]))
         ):
             side_copies.append(
                 pltpu.make_async_remote_copy(
@@ -255,7 +257,15 @@
             )
     for copy in side_copies:
         copy.start()
-    send_halo(0, solved_load)
+    copies[5].wait()
+    cut(inverse_v, inverse_parts)
+    for third in range(3):
+        await_stage(stage_recv, third, 0)
+        send_stage(third, 1)
+    send_halo(0, [times(inverse_parts, load[s], s) for s in range(2)])
+    for third in range(3):
+        await_stage(stage_recv, third, 1)
+        send_stage(third, 2)
     copies[6].wait()
     cut(schur_v, schur_parts)
     for copy in side_copies:
@@ -276,27 +286,42 @@
     ).astype(I32)
     owner = corner // OWN
     inner = corner - owner * OWN
-    third = inner // 8
-    pass_on(coarse_buf, 17, 0)
-    pass_on(buf1, 6, 1)
-    from_all(coarse_buf, 17, 0)
-
-    id_lanes = jnp.transpose(coarse_buf[:, 16, :])
-    id_rows[...] = id_lanes[0:48].astype(I32)
-    owned = jnp.where(id_lanes[48:49].astype(I32) == owner, 1.0, 0.0)
-    wanted = jnp.concatenate([inner % 8 + jnp.where(third == 2, 8, 0), 8 + inner % 8], axis=0)
-    owned = jnp.concatenate([owned, owned], axis=0)
+    third_of = inner // 8
+    wanted = jnp.concatenate(
+        [inner % 8 + jnp.where(third_of == 2, 8, 0), 8 + inner % 8], axis=0
+    )
+    slots = iota((1, LANES), 1)
+
+    def owned(third):
+        digits = [slots // 4**k % 4 for k in range(3)]
+        dz, dx, dy = (digits[ROUTES[third].index(axis)] for axis in range(3))
+        held = (z - dz) % 4 * 32 + (x - dx) % 4 * 8 + (y - dy) % 4 * 2 + (core + slots // 64) % 2
+        one = jnp.where(held == owner, 1.0, 0.0)
+        return jnp.concatenate([one, one], axis=0)
+
     pick = jnp.concatenate(
-        [jnp.where(wanted == r, owned, 0.0).astype(BF16) for r in range(16)], axis=1
+        [jnp.where(wanted == 8 * t + r, owned(t), 0.0).astype(BF16) for t in range(2) for r in range(8)],
+        axis=1,
     )
-    high, low = split(jnp.concatenate([coarse_buf[:, r, :] for r in range(16)], axis=0))
+    for third in range(3):
+        await_stage(stage_recv, third, 2)
+        forward(thirds[third], 8, third).start()
+    for third in range(3):
+        forward(thirds[third], 8, third).wait()
+        for stage in range(3):
+            await_stage(stage_send, third, stage)
+
+    id_rows[...] = jnp.transpose(buf1[:, 6, :])[0:48].astype(I32)
+    packed = [buf[:, r, :] for buf in (coarse_a, coarse_b) for r in range(8)]
+    high, low = split(jnp.concatenate(packed, axis=0))
     found = dot(pick, jnp.concatenate([high, low], axis=1))
     found = found[:, 0:LANES] + found[:, LANES : 2 * LANES]
-    lane96 = iota((96, LANES), 1)
-    from_a = take_lanes(found[0:96], jnp.minimum(lane96 + jnp.where(third == 1, 64, 0), LANES - 1))
-    from_t = take_lanes(found[96:192], jnp.minimum(lane96 + 8 * third, LANES - 1))
-    table[...] = jnp.where(lane96 < 64, from_a, jnp.where(lane96 < WIN, from_t, 0.0))
-    bases[...] = jnp.broadcast_to((owner - 1) * OWN, (96, LANES))
+    at = iota((96, LANES), 1) - 1
+    from_a = take_lanes(found[0:96], jnp.clip(at + jnp.where(third_of == 1, 64, 0), 0, LANES - 1))
+    from_t = take_lanes(found[96:192], jnp.clip(at + 8 * third_of, 0, LANES - 1))
+    window = jnp.where(at < 64, from_a, from_t)
+    table[...] = jnp.where((at >= 0) & (at < WIN), window, 0.0)
+    bases[...] = jnp.broadcast_to((owner - 1) * OWN - 1, (96, LANES))
 
     @pl.loop(0, 8)
     def _(e):
@@ -307,12 +332,9 @@
             out = pl.ds(pl.multiple_of(e * 96 + k * 16, 16), 16)
             for r in range(6):
                 place = jnp.broadcast_to(everyone[r], (16, LANES)) - base
-                place = jnp.where((place < 0) | (place >= WIN), LANES - 1, place)
-                top, rest = split(take_lanes(rows, place))
+                top, rest = split(take_lanes(rows, jnp.clip(place, 0, LANES - 1)))
                 operator[out, r * LANES : (r + 1) * LANES] = top
                 operator[out, (r + 6) * LANES : (r + 7) * LANES] = rest
-
-    from_all(buf1, 6, 1)
 
     def spread(buf):
         top, rest = split(jnp.concatenate([buf[:, r, :] for r in range(6)], axis=0))
@@ -349,41 +371,45 @@
     a = precondition(1, r0)
 
     buf2[0] = corner_rows(a)
-    to_all(buf2, 6, 2)
+    to_all(buf2, 6, 3)
     send_halo(2, [times(inverse_parts, a[s], s) for s in range(2)])
-    pass_on(buf2, 6, 2)
     solved_a = extended(2)
-    from_all(buf2, 6, 2)
-
-    q = [2.0 * v for v in jumped(add(spread(buf2), solved_a))]
+    from_all(buf2, 6, 3)
+
+    s_a = add(spread(buf2), solved_a)
+    q = [2.0 * v for v in jumped(s_a)]
     send_halo(3, [times(schur_parts, q[s], s) for s in range(2)])
     dots = as_row(products(r0, a), 0) + as_row(products(a, q), 1)
     w = [0.5 * v for v in jumped(extended(3))]
 
     buf3[0] = jnp.where(row8 == 6, dots, corner_rows(w))
-    to_all(buf3, 7, 3)
+    to_all(buf3, 7, 4)
     send_halo(4, [times(inverse_parts, w[s], s) for s in range(2)])
-    pass_on(buf3, 7, 3)
     solved_w = extended(4)
-    from_all(buf3, 7, 3)
-
-    u = [2.0 * v for v in jumped(add(spread(buf3), solved_w))]
+    from_all(buf3, 7, 4)
+
+    s_w = add(spread(buf3), solved_w)
     total = jnp.sum(buf3[:, 6, :], axis=0, keepdims=True)
     current, curvature = as_column(total, 0), as_column(total, 1)
     step0 = current / curvature
     r1 = [r0[s] - step0 * q[s] for s in range(2)]
     z1 = [a[s] - step0 * w[s] for s in range(2)]
+    s_z = [s_a[s + 1] - step0 * s_w[s + 1] for s in range(2)]
+    cross = 4.0 * (products(z1, s_a[1:3]) + products(a, s_z))
+    dots = as_row(products(r1, z1), 0) + as_row(4.0 * products(z1, s_z), 1) + as_row(cross, 2)
+    buf4[0] = jnp.where(row8 == 0, dots, 0.0)
+    for o in CHIPS:
+        for c in range(2):
+            if place_of(o) + c > 0:
+                pltpu.make_async_remote_copy(
+                    src_ref=buf4.at[0, pl.ds(0, 1)],
+                    dst_ref=buf4.at[place_of(o) + 64 * c, pl.ds(0, 1)],
+                    send_sem=all_send.at[5], recv_sem=all_recv.at[5],
+                    device_id=device(o, c), device_id_type=MESH,
+                ).start()
+    u = [2.0 * v for v in jumped(s_w)]
     image = [q[s] - step0 * u[s] for s in range(2)]
-    cross = products(z1, q) + products(a, image)
-    dots = as_row(products(r1, z1), 0) + as_row(products(z1, image), 1) + as_row(cross, 2)
-    buf4[0] = jnp.where(row8 == 0, dots, 0.0)
-    for to, o, c in EVERYONE:
-        pltpu.make_async_remote_copy(
-            src_ref=buf4.at[0, pl.ds(0, 1)], dst_ref=buf4.at[to, pl.ds(0, 1)],
-            send_sem=all_send.at[4], recv_sem=far_recv.at[4],
-            device_id=device(o, c), device_id_type=MESH,
-        ).start()
-    await_bytes(buf4.at[pl.ds(0, 127), pl.ds(0, 1)], far_recv.at[4])
+    await_bytes(buf4.at[pl.ds(0, 127), pl.ds(0, 1)], all_recv.at[5])
     total = jnp.sum(buf4[:, 0, :], axis=0, keepdims=True)
     following = as_column(total, 0)
     ratio = following / current
@@ -393,7 +419,7 @@
         mult_ref[:, s, :] = step0 * a[s] + step1 * (z1[s] + ratio * a[s])
         resid_ref[:, s, :] = r1[s] - step1 * (image[s] + ratio * q[s])
 
-    await_bytes(buf4.at[pl.ds(0, 127), pl.ds(0, 1)], all_send.at[4])
+    await_bytes(buf4.at[pl.ds(0, 127), pl.ds(0, 1)], all_send.at[5])
 
 
 def per_device(load, schur_inverse, schur, corner_map, corner_ids, coarse_inverse, partner):
@@ -416,8 +442,8 @@
             vmem((96, LANES), F32), vmem((96, LANES), I32), vmem((48, LANES), I32),
             vmem((768, 1536), BF16),
             vmem((5, 2, CASES, DOFS), F32), vmem((5, 2, CASES, DOFS), F32),
-            vmem((128, 24, LANES), F32), slots, slots, slots, slots,
-            dma((7,)), dma((5,)), dma((5,)), dma((5,)), dma((4,)), dma((4,)),
+            slots, slots, slots, slots, slots, slots,
+            dma((7,)), dma((3, 3)), dma((3, 3)), dma((6,)), dma((6,)), dma((5,)), dma((5,)),
             dma((7, 2)), dma((7, 2)),
         ],
         compiler_params=pltpu.CompilerParams(

time: 73.6 us -> 69.6 us (0.946)
  Pallas kernels: 69.8 us -> 65.8 us
    pallas_call x1, Pallas kernels: 69.8 us -> 65.8 us  [per_device(): pl.pallas_call(kernel, out_shape=(out, out), in_specs=[pl.BlockSpec(memor...]
where the time goes in v3:
time: 69.6 us; the launch traced here: 69.4 us
  Pallas kernels  65.8 us (95%)
  local copies, waits for them, and re-layouts  2.95 us (4%)
    pallas_call x1, Pallas kernels, per_device(): pl.pallas_call(kernel, out_shape=(out, out), in_specs=[pl.BlockSpec(memor...  65.8 us
    unnamed x2, local copies, waits for them, and re-layouts  2.95 us

profile of v3, /device:TPU:1, one launch (start us, length us, event | category | flops | bytes accessed | tf_op | source)
XLA Modules:
  0.0 69.4 jit_solution(12068081812127047727)
XLA Ops:
  0.6 65.8 %shard_map.86 = (f32[16,2,512]{2,1,0:T(2,128)}, f32[16,2,512]{2,1,0:T(2,128)}) custom-call(f32[16,2,512]{2,1,0:T(2,128)} %load_hbm.1, f32[2,512,512]{2,1,0:T(8,128)} %inverse_hbm.1, f32[2,512,512]{2,1,0:T(8,128)} %schur_hbm.1, f32[2,24,512]{2,1,0:T(8,128)} %map_hbm.1, s32[2,24]{1,0:T(2,128)} %ids_hbm.1, f32[24,72]{1,0:T(8,128)} %coarse_hbm.1, ...), custom_call_target="tpu_custom_call" | custom-call | tf_op jit(solution)/shard_map/pallas_call | solution.py:432
  66.5 1.5 %copy.11 = f32[16,2,512]{2,1,0:T(2,128)} copy(f32[16,2,512]{2,1,0:T(2,128)} %get-tuple-element.4) | data formatting | bytes 131072
  67.9 1.5 %copy.12 = f32[16,2,512]{2,1,0:T(2,128)} copy(f32[16,2,512]{2,1,0:T(2,128)} %get-tuple-element.5) | data formatting | bytes 131072

commit v4 on v3

--- a/solution.py
+++ b/solution.py
@@ -50,8 +50,10 @@
     mult_ref, resid_ref,
     load_v, inverse_v, schur_v, map_v, ids_v, coarse_v, partner_v,
     inverse_parts, schur_parts, map_high, map_low, map_side, id_side,
-    table, bases, id_rows, operator, field, halo, coarse_a, coarse_b, buf1, buf2, buf3, buf4,
+    partner_side, schur_side, side_parts, table, bases, id_rows, operator, operator_wide,
+    field, halo, halo_wide, coarse_a, coarse_b, buf1, buf2, buf3, buf4,
     in_sem, stage_send, stage_recv, all_send, all_recv, fwd_send, fwd_recv, halo_send, halo_recv,
+    side_send, side_recv,
 ):
     me = lax.axis_index("sub")
     core, chip = me % 2, me // 2
@@ -90,6 +92,8 @@
     for copy in copies[:5]:
         copy.wait()
     gap = jnp.zeros((8, DOFS), F32)
+    map_high[192:256] = jnp.zeros((64, DOFS), BF16)
+    map_low[192:256] = jnp.zeros((64, DOFS), BF16)
     own_maps = [map_v[s] for s in range(2)]
     for s in range(2):
         high, low = split(jnp.concatenate([own_maps[s], gap], axis=0))
@@ -106,25 +110,23 @@
     second = jnp.where(lane8 >= 80, pltpu.roll(m2, 16, 1), second)
     coarse_b[0] = jnp.where(lane8 >= 88, 0.0, second)
 
-    flat = partner_v[...] - (2 * me - 1) * DOFS
-    mate_block = flat // LANES
-    mate_lane = flat % LANES
+    def jump(window, partners):
+        columns = []
+        for t in range(4):
+            at = slice(t * LANES, (t + 1) * LANES)
+            flat = jnp.broadcast_to(partners[:, at], (CASES, LANES))
+            lanes, block = flat % LANES, flat // LANES
+            mate = jnp.zeros((CASES, LANES), F32)
+            for b in range(12):
+                source = window[b // 4][:, b % 4 * LANES : (b % 4 + 1) * LANES]
+                mate = jnp.where(block == b, take_lanes(source, lanes), mate)
+            columns.append(window[1][:, at] - mate)
+        return jnp.concatenate(columns, axis=1)
+
+    own_partners = [partner_v[s : s + 1] - (2 * me + s - 1) * DOFS for s in range(2)]
 
     def jumped(extended):
-        out = []
-        for s in range(2):
-            columns = []
-            for t in range(4):
-                at = slice(t * LANES, (t + 1) * LANES)
-                lanes = jnp.broadcast_to(mate_lane[s : s + 1, at], (CASES, LANES))
-                block = jnp.broadcast_to(mate_block[s : s + 1, at], (CASES, LANES))
-                mate = jnp.zeros((CASES, LANES), F32)
-                for b in range(4 * s, 4 * s + 12):
-                    source = extended[b // 4][:, b % 4 * LANES : (b % 4 + 1) * LANES]
-                    mate = jnp.where(block == b, take_lanes(source, lanes), mate)
-                columns.append(extended[s + 1][:, at] - mate)
-            out.append(jnp.concatenate(columns, axis=1))
-        return out
+        return [jump(extended[s : s + 3], own_partners[s]) for s in range(2)]
 
     def corner_rows(pair):
         tiles = []
@@ -208,10 +210,10 @@
                 device_id=device(o, 0), device_id_type=MESH,
             ).start()
 
-    def forward(buf, rows, n):
+    def forward(buf, rows, n, first=0, count=64):
         return pltpu.make_async_remote_copy(
-            src_ref=buf.at[pl.ds(0, 64), pl.ds(0, rows)],
-            dst_ref=buf.at[pl.ds(64, 64), pl.ds(0, rows)],
+            src_ref=buf.at[pl.ds(first, count), pl.ds(0, rows)],
+            dst_ref=buf.at[pl.ds(64 + first, count), pl.ds(0, rows)],
             send_sem=fwd_send.at[n], recv_sem=fwd_recv.at[n],
             device_id=device((0, 0, 0), 1), device_id_type=MESH,
         )
@@ -244,17 +246,33 @@
     pl.semaphore_wait(barrier, len(partners))
     for third in range(3):
         send_stage(third, 0)
-    side_copies = []
-    for i, (dev, near) in enumerate(((right, 1), (left, 0))):
-        for n, (src, dst) in enumerate(
-            ((map_v.at[near], map_side.at[i]), (buf1.at[0, pl.ds(6, 1)], id_side.at[i]))
-        ):
-            side_copies.append(
-                pltpu.make_async_remote_copy(
-                    src_ref=src, dst_ref=dst, send_sem=halo_send.at[5 + n, i],
-                    recv_sem=halo_recv.at[5 + n, i], device_id=(dev,), device_id_type=MESH,
+    def beside(copies):
+        made = []
+        for i, dev in enumerate((right, left)):
+            for src, dst, n in copies(i):
+                made.append(
+                    pltpu.make_async_remote_copy(
+                        src_ref=src, dst_ref=dst, send_sem=side_send.at[n, i],
+                        recv_sem=side_recv.at[n, i], device_id=(dev,), device_id_type=MESH,
+                    )
                 )
-            )
+        return made
+
+    side_copies = beside(
+        lambda i: (
+            (map_v, map_side.at[i], 0),
+            (buf1.at[0, pl.ds(6, 1)], id_side.at[i], 1),
+            (partner_v, partner_side.at[i], 2),
+        )
+    )
+    def upper(block):
+        return pl.ds(block * LANES, LANES), pl.ds(block * LANES, DOFS - block * LANES)
+
+    schur_copies = [
+        beside(lambda i: ((schur_v.at[1 - i, *upper(b)], schur_side.at[i, *upper(b)], 4 + b),))
+        for b in range(4)
+    ]
+    wide_copies = beside(lambda i: ((field.at[2], halo_wide.at[i], 3),))
     for copy in side_copies:
         copy.start()
     copies[5].wait()
@@ -266,14 +284,15 @@
     for third in range(3):
         await_stage(stage_recv, third, 1)
         send_stage(third, 2)
+        forward(thirds[third], 8, 2 * third, 0, 16).start()
     copies[6].wait()
     cut(schur_v, schur_parts)
     for copy in side_copies:
         copy.wait()
-    for i in range(2):
-        high, low = split(jnp.concatenate([map_side[i], gap], axis=0))
-        map_high[96 * i : 96 * i + 32] = high
-        map_low[96 * i : 96 * i + 32] = low
+    for first, i, side in ((0, 0, 1), (96, 1, 0), (128, 0, 0), (160, 1, 1)):
+        high, low = split(jnp.concatenate([map_side[i, side], gap], axis=0))
+        map_high[first : first + 32] = high
+        map_low[first : first + 32] = low
     row48 = iota((48, LANES), 0)
     lane48 = iota((48, LANES), 1)
 
@@ -281,8 +300,9 @@
         kept = jnp.where(row48 == lane48, jnp.broadcast_to(row, (48, LANES)), 0.0)
         return jnp.sum(kept, axis=1, keepdims=True)
 
+    before, after = id_column(id_side[0]), id_column(id_side[1])
     corner = jnp.concatenate(
-        [id_column(id_side[0])[24:48], id_column(ids), id_column(id_side[1])[0:24]], axis=0
+        [before[24:48], id_column(ids), after[0:24], before[0:24], after[24:48]], axis=0
     ).astype(I32)
     owner = corner // OWN
     inner = corner - owner * OWN
@@ -305,97 +325,153 @@
     )
     for third in range(3):
         await_stage(stage_recv, third, 2)
-        forward(thirds[third], 8, third).start()
-    for third in range(3):
-        forward(thirds[third], 8, third).wait()
-        for stage in range(3):
-            await_stage(stage_send, third, stage)
-
-    id_rows[...] = jnp.transpose(buf1[:, 6, :])[0:48].astype(I32)
+        forward(thirds[third], 8, 2 * third + 1, 16, 48).start()
+
+    for copy in itertools.chain(*schur_copies[:1]):
+        copy.start()
+
+    def await_forward(third):
+        forward(thirds[third], 8, 2 * third, 0, 16).wait()
+        forward(thirds[third], 8, 2 * third + 1, 16, 48).wait()
+
+    await_forward(0)
+    await_forward(1)
     packed = [buf[:, r, :] for buf in (coarse_a, coarse_b) for r in range(8)]
     high, low = split(jnp.concatenate(packed, axis=0))
     found = dot(pick, jnp.concatenate([high, low], axis=1))
     found = found[:, 0:LANES] + found[:, LANES : 2 * LANES]
-    at = iota((96, LANES), 1) - 1
-    from_a = take_lanes(found[0:96], jnp.clip(at + jnp.where(third_of == 1, 64, 0), 0, LANES - 1))
-    from_t = take_lanes(found[96:192], jnp.clip(at + 8 * third_of, 0, LANES - 1))
+    at = iota((144, LANES), 1) - 1
+    from_a = take_lanes(found[0:144], jnp.clip(at + jnp.where(third_of == 1, 64, 0), 0, LANES - 1))
+    from_t = take_lanes(found[144:288], jnp.clip(at + 8 * third_of, 0, LANES - 1))
     window = jnp.where(at < 64, from_a, from_t)
     table[...] = jnp.where((at >= 0) & (at < WIN), window, 0.0)
-    bases[...] = jnp.broadcast_to((owner - 1) * OWN - 1, (96, LANES))
-
-    @pl.loop(0, 8)
-    def _(e):
-        everyone = [id_rows[pl.ds(8 * r + e, 1), :] for r in range(6)]
-        for k in range(6):
-            rows = table[16 * k : 16 * k + 16]
-            base = bases[16 * k : 16 * k + 16]
-            out = pl.ds(pl.multiple_of(e * 96 + k * 16, 16), 16)
-            for r in range(6):
-                place = jnp.broadcast_to(everyone[r], (16, LANES)) - base
-                top, rest = split(take_lanes(rows, jnp.clip(place, 0, LANES - 1)))
-                operator[out, r * LANES : (r + 1) * LANES] = top
-                operator[out, (r + 6) * LANES : (r + 7) * LANES] = rest
-
-    def spread(buf):
+    bases[...] = jnp.broadcast_to((owner - 1) * OWN - 1, (144, LANES))
+
+    def build(out_ref, first, count):
+        @pl.loop(0, 8)
+        def _(e):
+            everyone = [id_rows[pl.ds(8 * r + e, 1), :] for r in range(6)]
+            for k in range(0, count, 16):
+                rows = table[first + k : first + k + 16]
+                base = bases[first + k : first + k + 16]
+                out = pl.ds(pl.multiple_of(e * count + k, 16), 16)
+                for r in range(6):
+                    place = jnp.broadcast_to(everyone[r], (16, LANES)) - base
+                    top, rest = split(take_lanes(rows, jnp.clip(place, 0, LANES - 1)))
+                    out_ref[out, r * LANES : (r + 1) * LANES] = top
+                    out_ref[out, (r + 6) * LANES : (r + 7) * LANES] = rest
+
+    await_forward(2)
+    id_rows[...] = jnp.transpose(buf1[:, 6, :])[0:48].astype(I32)
+    build(operator, 0, 96)
+    for third in range(3):
+        for stage in range(3):
+            await_stage(stage_send, third, stage)
+
+    def gathered(buf):
         top, rest = split(jnp.concatenate([buf[:, r, :] for r in range(6)], axis=0))
         both = jnp.concatenate([top, rest], axis=1)
-        product = dot(operator[...], jnp.concatenate([both, both], axis=0))
-        solved = jnp.zeros((96, 2 * LANES), F32)
-        lanes = iota((96, 2 * LANES), 1) % LANES // 16
+        return jnp.concatenate([both, both], axis=0)
+
+    def spread(everyone, rows_ref, subs, first):
+        count = 24 * subs
+        product = dot(rows_ref[...], everyone)
+        solved = jnp.zeros((count, 2 * LANES), F32)
+        lanes = iota((count, 2 * LANES), 1) % LANES // 16
         for e in range(8):
-            solved = jnp.where(lanes == e, product[96 * e : 96 * e + 96], solved)
+            solved = jnp.where(lanes == e, product[count * e : count * e + count], solved)
         solved = solved[:, 0:LANES] + solved[:, LANES : 2 * LANES]
-        zero = jnp.zeros((8, LANES), F32)
         padded = []
         for j in range(4):
-            padded += [solved[24 * j : 24 * j + 24], zero]
+            if j < subs:
+                padded += [solved[24 * j : 24 * j + 24], jnp.zeros((8, LANES), F32)]
+            else:
+                padded += [jnp.zeros((32, LANES), F32)]
         turned = jnp.transpose(jnp.concatenate(padded, axis=0))
         by_case = turned[0:CASES]
         for e in range(1, 8):
             by_case = by_case + turned[CASES * e : CASES * e + CASES]
         stack = []
-        for j in range(4):
+        for j in range(subs):
             stack += list(split(jnp.where(lane16 // 32 == j, by_case, 0.0)))
         stack = jnp.concatenate(stack, axis=0)
-        product = dot(stack, map_high[...]) + dot(stack, map_low[...])
-        return [product[32 * j : 32 * j + 16] + product[32 * j + 16 : 32 * j + 32] for j in range(4)]
+        maps = slice(first, first + LANES)
+        product = dot(stack, map_high[maps]) + dot(stack, map_low[maps])
+        return [product[32 * j : 32 * j + 16] + product[32 * j + 16 : 32 * j + 32] for j in range(subs)]
+
+    def around(buf):
+        return spread(gathered(buf), operator, 4, 0)
 
     def add(first, second):
         return [a + b for a, b in zip(first, second)]
 
-    def precondition(n, pair):
-        send_halo(n, [times(schur_parts, pair[s], s) for s in range(2)])
-        return [0.5 * v for v in jumped(extended(n))]
-
-    r0 = jumped(add(spread(buf1), extended(0)))
-    a = precondition(1, r0)
+    r0 = jumped(add(around(buf1), extended(0)))
+    send_halo(1, [times(schur_parts, r0[s], s) for s in range(2)])
+    for copy in itertools.chain(*schur_copies[1:]):
+        copy.start()
+    a = [0.5 * v for v in jumped(extended(1))]
 
     buf2[0] = corner_rows(a)
-    to_all(buf2, 6, 3)
-    send_halo(2, [times(inverse_parts, a[s], s) for s in range(2)])
-    solved_a = extended(2)
-    from_all(buf2, 6, 3)
-
-    s_a = add(spread(buf2), solved_a)
-    q = [2.0 * v for v in jumped(s_a)]
-    send_halo(3, [times(schur_parts, q[s], s) for s in range(2)])
+    to_all(buf2, 6, 6)
+    field[2, 0] = times(inverse_parts, a[0], 0)
+    field[2, 1] = times(inverse_parts, a[1], 1)
+    for copy in wide_copies:
+        copy.start()
+    build(operator_wide, 96, 48)
+    for copy in itertools.chain(*schur_copies):
+        copy.wait()
+
+    @pl.loop(0, 2)
+    def _(i):
+        for b in range(4):
+            for c in range(4):
+                first, last = min(b, c) * LANES, max(b, c) * LANES
+                block = schur_side[i, first : first + LANES, last : last + LANES]
+                top, rest = split(block if b <= c else jnp.transpose(block))
+                columns = slice(c * LANES, (c + 1) * LANES)
+                side_parts[i, b * LANES : (b + 1) * LANES, columns] = top
+                side_parts[i, DOFS + b * LANES : DOFS + (b + 1) * LANES, columns] = rest
+
+    for copy in wide_copies:
+        copy.wait()
+    from_all(buf2, 6, 6)
+
+    everyone = gathered(buf2)
+    near = spread(everyone, operator, 4, 0)
+    near = add(near, [halo_wide[0, 1], field[2, 0], field[2, 1], halo_wide[1, 0]])
+    far = add(spread(everyone, operator_wide, 2, 128), [halo_wide[0, 0], halo_wide[1, 1]])
+    s_a = [far[0], *near, far[1]]
+    side_partners = [
+        partner_side[0][1:2] - (2 * me - 2) * DOFS, partner_side[1][0:1] - (2 * me + 1) * DOFS
+    ]
+    partners4 = [side_partners[0], *own_partners, side_partners[1]]
+    q4 = [2.0 * jump(s_a[j : j + 3], partners4[j]) for j in range(4)]
+    w = [
+        0.5 * v
+        for v in jumped(
+            [
+                times(side_parts, q4[0], 0), times(schur_parts, q4[1], 0),
+                times(schur_parts, q4[2], 1), times(side_parts, q4[3], 1),
+            ]
+        )
+    ]
+    s_a, q = s_a[2:4], q4[1:3]
     dots = as_row(products(r0, a), 0) + as_row(products(a, q), 1)
-    w = [0.5 * v for v in jumped(extended(3))]
 
     buf3[0] = jnp.where(row8 == 6, dots, corner_rows(w))
-    to_all(buf3, 7, 4)
+    to_all(buf3, 7, 7)
     send_halo(4, [times(inverse_parts, w[s], s) for s in range(2)])
     solved_w = extended(4)
-    from_all(buf3, 7, 4)
-
-    s_w = add(spread(buf3), solved_w)
+    from_all(buf3, 7, 7)
+
+    s_w = add(around(buf3), solved_w)
     total = jnp.sum(buf3[:, 6, :], axis=0, keepdims=True)
     current, curvature = as_column(total, 0), as_column(total, 1)
     step0 = current / curvature
     r1 = [r0[s] - step0 * q[s] for s in range(2)]
     z1 = [a[s] - step0 * w[s] for s in range(2)]
-    s_z = [s_a[s + 1] - step0 * s_w[s + 1] for s in range(2)]
-    cross = 4.0 * (products(z1, s_a[1:3]) + products(a, s_z))
+    s_z = [s_a[s] - step0 * s_w[s + 1] for s in range(2)]
+    cross = 4.0 * (products(z1, s_a) + products(a, s_z))
     dots = as_row(products(r1, z1), 0) + as_row(4.0 * products(z1, s_z), 1) + as_row(cross, 2)
     buf4[0] = jnp.where(row8 == 0, dots, 0.0)
     for o in CHIPS:
@@ -404,12 +480,12 @@
                 pltpu.make_async_remote_copy(
                     src_ref=buf4.at[0, pl.ds(0, 1)],
                     dst_ref=buf4.at[place_of(o) + 64 * c, pl.ds(0, 1)],
-                    send_sem=all_send.at[5], recv_sem=all_recv.at[5],
+                    send_sem=all_send.at[8], recv_sem=all_recv.at[8],
                     device_id=device(o, c), device_id_type=MESH,
                 ).start()
     u = [2.0 * v for v in jumped(s_w)]
     image = [q[s] - step0 * u[s] for s in range(2)]
-    await_bytes(buf4.at[pl.ds(0, 127), pl.ds(0, 1)], all_recv.at[5])
+    await_bytes(buf4.at[pl.ds(0, 127), pl.ds(0, 1)], all_recv.at[8])
     total = jnp.sum(buf4[:, 0, :], axis=0, keepdims=True)
     following = as_column(total, 0)
     ratio = following / current
@@ -419,7 +495,7 @@
         mult_ref[:, s, :] = step0 * a[s] + step1 * (z1[s] + ratio * a[s])
         resid_ref[:, s, :] = r1[s] - step1 * (image[s] + ratio * q[s])
 
-    await_bytes(buf4.at[pl.ds(0, 127), pl.ds(0, 1)], all_send.at[5])
+    await_bytes(buf4.at[pl.ds(0, 127), pl.ds(0, 1)], all_send.at[8])
 
 
 def per_device(load, schur_inverse, schur, corner_map, corner_ids, coarse_inverse, partner):
@@ -437,14 +513,16 @@
         scratch_shapes=[
             *(vmem(v.shape, v.dtype) for v in inputs),
             parts, parts,
-            vmem((128, DOFS), BF16), vmem((128, DOFS), BF16),
-            vmem((2, CORNERS, DOFS), F32), vmem((2, 1, LANES), F32),
-            vmem((96, LANES), F32), vmem((96, LANES), I32), vmem((48, LANES), I32),
-            vmem((768, 1536), BF16),
+            vmem((256, DOFS), BF16), vmem((256, DOFS), BF16),
+            vmem((2, 2, CORNERS, DOFS), F32), vmem((2, 1, LANES), F32),
+            vmem((2, 2, DOFS), I32), vmem((2, DOFS, DOFS), F32), parts,
+            vmem((144, LANES), F32), vmem((144, LANES), I32), vmem((48, LANES), I32),
+            vmem((768, 1536), BF16), vmem((384, 1536), BF16),
             vmem((5, 2, CASES, DOFS), F32), vmem((5, 2, CASES, DOFS), F32),
+            vmem((2, 2, CASES, DOFS), F32),
             slots, slots, slots, slots, slots, slots,
-            dma((7,)), dma((3, 3)), dma((3, 3)), dma((6,)), dma((6,)), dma((5,)), dma((5,)),
-            dma((7, 2)), dma((7, 2)),
+            dma((7,)), dma((3, 3)), dma((3, 3)), dma((9,)), dma((9,)), dma((8,)), dma((8,)),
+            dma((5, 2)), dma((5, 2)), dma((8, 2)), dma((8, 2)),
         ],
         compiler_params=pltpu.CompilerParams(
             collective_id=0, has_side_effects=True, vmem_limit_bytes=63 << 20

time: 69.6 us -> 68.1 us (0.978)
  Pallas kernels: 65.8 us -> 64.3 us
    pallas_call x1, Pallas kernels: 65.8 us -> 64.3 us  [per_device(): pl.pallas_call(kernel, out_shape=(out, out), in_specs=[pl.BlockSpec(memor...]
where the time goes in v4:
time: 68.1 us; the launch traced here: 67.9 us
  Pallas kernels  64.3 us (94%)
  local copies, waits for them, and re-layouts  2.95 us (4%)
    pallas_call x1, Pallas kernels, per_device(): pl.pallas_call(kernel, out_shape=(out, out), in_specs=[pl.BlockSpec(memor...  64.3 us
    unnamed x2, local copies, waits for them, and re-layouts  2.95 us

profile of v4, /device:TPU:1, one launch (start us, length us, event | category | flops | bytes accessed | tf_op | source)
XLA Modules:
  0.0 67.9 jit_solution(16586364444790962521)
XLA Ops:
  0.6 64.3 %shard_map.86 = (f32[16,2,512]{2,1,0:T(2,128)}, f32[16,2,512]{2,1,0:T(2,128)}) custom-call(f32[16,2,512]{2,1,0:T(2,128)} %load_hbm.1, f32[2,512,512]{2,1,0:T(8,128)} %inverse_hbm.1, f32[2,512,512]{2,1,0:T(8,128)} %schur_hbm.1, f32[2,24,512]{2,1,0:T(8,128)} %map_hbm.1, s32[2,24]{1,0:T(2,128)} %ids_hbm.1, f32[24,72]{1,0:T(8,128)} %coarse_hbm.1, ...), custom_call_target="tpu_custom_call" | custom-call | tf_op jit(solution)/shard_map/pallas_call | solution.py:508
  65.0 1.5 %copy.11 = f32[16,2,512]{2,1,0:T(2,128)} copy(f32[16,2,512]{2,1,0:T(2,128)} %get-tuple-element.4) | data formatting | bytes 131072
  66.5 1.5 %copy.12 = f32[16,2,512]{2,1,0:T(2,128)} copy(f32[16,2,512]{2,1,0:T(2,128)} %get-tuple-element.5) | data formatting | bytes 131072

commit v5 on v4

--- a/solution.py
+++ b/solution.py
@@ -50,7 +50,7 @@
     mult_ref, resid_ref,
     load_v, inverse_v, schur_v, map_v, ids_v, coarse_v, partner_v,
     inverse_parts, schur_parts, map_high, map_low, map_side, id_side,
-    partner_side, schur_side, side_parts, table, bases, id_rows, operator, operator_wide,
+    partner_side, schur_side, side_parts, table, bases, id_rows, operator,
     field, halo, halo_wide, coarse_a, coarse_b, buf1, buf2, buf3, buf4,
     in_sem, stage_send, stage_recv, all_send, all_recv, fwd_send, fwd_recv, halo_send, halo_recv,
     side_send, side_recv,
@@ -97,8 +97,8 @@
     own_maps = [map_v[s] for s in range(2)]
     for s in range(2):
         high, low = split(jnp.concatenate([own_maps[s], gap], axis=0))
-        map_high[32 * (s + 1) : 32 * (s + 2)] = high
-        map_low[32 * (s + 1) : 32 * (s + 2)] = low
+        map_high[32 * s : 32 * s + 32] = high
+        map_low[32 * s : 32 * s + 32] = low
 
     coarse = jnp.concatenate([coarse_v[...], jnp.zeros((OWN, LANES - WIN), F32)], axis=1)
     m0, m1, m2 = coarse[0:8], coarse[8:16], coarse[16:24]
@@ -133,7 +133,7 @@
         for s in range(2):
             high, low = split(pair[s])
             both = jnp.concatenate([high] * 8 + [low] * 8, axis=0)
-            at = slice(32 * (s + 1), 32 * (s + 2))
+            at = slice(32 * s, 32 * s + 32)
             maps = jnp.concatenate([map_high[at], map_low[at]], axis=0)
             product = lax.dot_general(
                 maps, both, (((1,), (1,)), ((), ())), preferred_element_type=F32
@@ -289,7 +289,7 @@
     cut(schur_v, schur_parts)
     for copy in side_copies:
         copy.wait()
-    for first, i, side in ((0, 0, 1), (96, 1, 0), (128, 0, 0), (160, 1, 1)):
+    for first, i, side in ((64, 0, 1), (96, 1, 0), (128, 0, 0), (160, 1, 1)):
         high, low = split(jnp.concatenate([map_side[i, side], gap], axis=0))
         map_high[first : first + 32] = high
         map_low[first : first + 32] = low
@@ -302,7 +302,7 @@
 
     before, after = id_column(id_side[0]), id_column(id_side[1])
     corner = jnp.concatenate(
-        [before[24:48], id_column(ids), after[0:24], before[0:24], after[24:48]], axis=0
+        [id_column(ids), before[24:48], after[0:24], before[0:24], after[24:48]], axis=0
     ).astype(I32)
     owner = corner // OWN
     inner = corner - owner * OWN
@@ -347,23 +347,23 @@
     table[...] = jnp.where((at >= 0) & (at < WIN), window, 0.0)
     bases[...] = jnp.broadcast_to((owner - 1) * OWN - 1, (144, LANES))
 
-    def build(out_ref, first, count):
+    def build(first, count):
         @pl.loop(0, 8)
         def _(e):
             everyone = [id_rows[pl.ds(8 * r + e, 1), :] for r in range(6)]
-            for k in range(0, count, 16):
-                rows = table[first + k : first + k + 16]
-                base = bases[first + k : first + k + 16]
-                out = pl.ds(pl.multiple_of(e * count + k, 16), 16)
+            for k in range(first, first + count, 16):
+                rows = table[k : k + 16]
+                base = bases[k : k + 16]
+                out = pl.ds(pl.multiple_of(k // 48 * 384 + e * 48 + k % 48, 16), 16)
                 for r in range(6):
                     place = jnp.broadcast_to(everyone[r], (16, LANES)) - base
                     top, rest = split(take_lanes(rows, jnp.clip(place, 0, LANES - 1)))
-                    out_ref[out, r * LANES : (r + 1) * LANES] = top
-                    out_ref[out, (r + 6) * LANES : (r + 7) * LANES] = rest
+                    operator[out, r * LANES : (r + 1) * LANES] = top
+                    operator[out, (r + 6) * LANES : (r + 7) * LANES] = rest
 
     await_forward(2)
     id_rows[...] = jnp.transpose(buf1[:, 6, :])[0:48].astype(I32)
-    build(operator, 0, 96)
+    build(0, 96)
     for third in range(3):
         for stage in range(3):
             await_stage(stage_send, third, stage)
@@ -373,39 +373,44 @@
         both = jnp.concatenate([top, rest], axis=1)
         return jnp.concatenate([both, both], axis=0)
 
-    def spread(everyone, rows_ref, subs, first):
-        count = 24 * subs
-        product = dot(rows_ref[...], everyone)
-        solved = jnp.zeros((count, 2 * LANES), F32)
-        lanes = iota((count, 2 * LANES), 1) % LANES // 16
-        for e in range(8):
-            solved = jnp.where(lanes == e, product[count * e : count * e + count], solved)
-        solved = solved[:, 0:LANES] + solved[:, LANES : 2 * LANES]
+    def spread(everyone, first, count):
         padded = []
-        for j in range(4):
-            if j < subs:
-                padded += [solved[24 * j : 24 * j + 24], jnp.zeros((8, LANES), F32)]
-            else:
-                padded += [jnp.zeros((32, LANES), F32)]
+        lanes = iota((48, 2 * LANES), 1) % LANES // 16
+        for pair in range(first, first + count):
+            solved = jnp.zeros((48, 2 * LANES), F32)
+            for half in range(2):
+                at = 384 * pair + 192 * half
+                product = dot(operator[at : at + 192], everyone)
+                for e in range(4):
+                    solved = jnp.where(lanes == 4 * half + e, product[48 * e : 48 * e + 48], solved)
+            solved = solved[:, 0:LANES] + solved[:, LANES : 2 * LANES]
+            zero = jnp.zeros((8, LANES), F32)
+            padded += [solved[0:24], zero, solved[24:48], zero]
+        if count == 1:
+            padded.append(jnp.zeros((64, LANES), F32))
         turned = jnp.transpose(jnp.concatenate(padded, axis=0))
         by_case = turned[0:CASES]
         for e in range(1, 8):
             by_case = by_case + turned[CASES * e : CASES * e + CASES]
         stack = []
-        for j in range(subs):
+        for j in range(2 * count):
             stack += list(split(jnp.where(lane16 // 32 == j, by_case, 0.0)))
         stack = jnp.concatenate(stack, axis=0)
-        maps = slice(first, first + LANES)
+        maps = slice(64 * first, 64 * first + LANES)
         product = dot(stack, map_high[maps]) + dot(stack, map_low[maps])
-        return [product[32 * j : 32 * j + 16] + product[32 * j + 16 : 32 * j + 32] for j in range(subs)]
-
-    def around(buf):
-        return spread(gathered(buf), operator, 4, 0)
+        return [
+            product[32 * j : 32 * j + 16] + product[32 * j + 16 : 32 * j + 32]
+            for j in range(2 * count)
+        ]
+
+    def around(everyone):
+        own0, own1, before, after = spread(everyone, 0, 2)
+        return [before, own0, own1, after]
 
     def add(first, second):
         return [a + b for a, b in zip(first, second)]
 
-    r0 = jumped(add(around(buf1), extended(0)))
+    r0 = jumped(add(around(gathered(buf1)), extended(0)))
     send_halo(1, [times(schur_parts, r0[s], s) for s in range(2)])
     for copy in itertools.chain(*schur_copies[1:]):
         copy.start()
@@ -417,7 +422,7 @@
     field[2, 1] = times(inverse_parts, a[1], 1)
     for copy in wide_copies:
         copy.start()
-    build(operator_wide, 96, 48)
+    build(96, 48)
     for copy in itertools.chain(*schur_copies):
         copy.wait()
 
@@ -437,9 +442,9 @@
     from_all(buf2, 6, 6)
 
     everyone = gathered(buf2)
-    near = spread(everyone, operator, 4, 0)
+    near = around(everyone)
     near = add(near, [halo_wide[0, 1], field[2, 0], field[2, 1], halo_wide[1, 0]])
-    far = add(spread(everyone, operator_wide, 2, 128), [halo_wide[0, 0], halo_wide[1, 1]])
+    far = add(spread(everyone, 2, 1), [halo_wide[0, 0], halo_wide[1, 1]])
     s_a = [far[0], *near, far[1]]
     side_partners = [
         partner_side[0][1:2] - (2 * me - 2) * DOFS, partner_side[1][0:1] - (2 * me + 1) * DOFS
@@ -464,13 +469,14 @@
     solved_w = extended(4)
     from_all(buf3, 7, 7)
 
-    s_w = add(around(buf3), solved_w)
+    everyone = gathered(buf3)
+    s_w = add(spread(everyone, 0, 1), solved_w[1:3])
     total = jnp.sum(buf3[:, 6, :], axis=0, keepdims=True)
     current, curvature = as_column(total, 0), as_column(total, 1)
     step0 = current / curvature
     r1 = [r0[s] - step0 * q[s] for s in range(2)]
     z1 = [a[s] - step0 * w[s] for s in range(2)]
-    s_z = [s_a[s] - step0 * s_w[s + 1] for s in range(2)]
+    s_z = [s_a[s] - step0 * s_w[s] for s in range(2)]
     cross = 4.0 * (products(z1, s_a) + products(a, s_z))
     dots = as_row(products(r1, z1), 0) + as_row(4.0 * products(z1, s_z), 1) + as_row(cross, 2)
     buf4[0] = jnp.where(row8 == 0, dots, 0.0)
@@ -483,7 +489,8 @@
                     send_sem=all_send.at[8], recv_sem=all_recv.at[8],
                     device_id=device(o, c), device_id_type=MESH,
                 ).start()
-    u = [2.0 * v for v in jumped(s_w)]
+    before, after = add(spread(everyone, 1, 1), [solved_w[0], solved_w[3]])
+    u = [2.0 * v for v in jumped([before, *s_w, after])]
     image = [q[s] - step0 * u[s] for s in range(2)]
     await_bytes(buf4.at[pl.ds(0, 127), pl.ds(0, 1)], all_recv.at[8])
     total = jnp.sum(buf4[:, 0, :], axis=0, keepdims=True)
@@ -517,7 +524,7 @@
             vmem((2, 2, CORNERS, DOFS), F32), vmem((2, 1, LANES), F32),
             vmem((2, 2, DOFS), I32), vmem((2, DOFS, DOFS), F32), parts,
             vmem((144, LANES), F32), vmem((144, LANES), I32), vmem((48, LANES), I32),
-            vmem((768, 1536), BF16), vmem((384, 1536), BF16),
+            vmem((1152, 1536), BF16),
             vmem((5, 2, CASES, DOFS), F32), vmem((5, 2, CASES, DOFS), F32),
             vmem((2, 2, CASES, DOFS), F32),
             slots, slots, slots, slots, slots, slots,

time: 68.1 us -> 66.5 us (0.977)
  Pallas kernels: 64.3 us -> 62.7 us
    pallas_call x1, Pallas kernels: 64.3 us -> 62.7 us  [per_device(): pl.pallas_call(kernel, out_shape=(out, out), in_specs=[pl.BlockSpec(memor...]
where the time goes in v5:
time: 66.5 us; the launch traced here: 66.3 us
  Pallas kernels  62.7 us (94%)
  local copies, waits for them, and re-layouts  2.95 us (4%)
    pallas_call x1, Pallas kernels, per_device(): pl.pallas_call(kernel, out_shape=(out, out), in_specs=[pl.BlockSpec(memor...  62.7 us
    unnamed x2, local copies, waits for them, and re-layouts  2.95 us

profile of v5, /device:TPU:1, one launch (start us, length us, event | category | flops | bytes accessed | tf_op | source)
XLA Modules:
  0.0 66.3 jit_solution(14436626989494911893)
XLA Ops:
  0.6 62.7 %shard_map.86 = (f32[16,2,512]{2,1,0:T(2,128)}, f32[16,2,512]{2,1,0:T(2,128)}) custom-call(f32[16,2,512]{2,1,0:T(2,128)} %load_hbm.1, f32[2,512,512]{2,1,0:T(8,128)} %inverse_hbm.1, f32[2,512,512]{2,1,0:T(8,128)} %schur_hbm.1, f32[2,24,512]{2,1,0:T(8,128)} %map_hbm.1, s32[2,24]{1,0:T(2,128)} %ids_hbm.1, f32[24,72]{1,0:T(8,128)} %coarse_hbm.1, ...), custom_call_target="tpu_custom_call" | custom-call | tf_op jit(solution)/shard_map/pallas_call | solution.py:515
  63.4 1.5 %copy.11 = f32[16,2,512]{2,1,0:T(2,128)} copy(f32[16,2,512]{2,1,0:T(2,128)} %get-tuple-element.4) | data formatting | bytes 131072
  64.8 1.5 %copy.12 = f32[16,2,512]{2,1,0:T(2,128)} copy(f32[16,2,512]{2,1,0:T(2,128)} %get-tuple-element.5) | data formatting | bytes 131072

commit v6 on v5

--- a/solution.py
+++ b/solution.py
@@ -348,7 +348,7 @@
     bases[...] = jnp.broadcast_to((owner - 1) * OWN - 1, (144, LANES))
 
     def build(first, count):
-        @pl.loop(0, 8)
+        @pl.loop(0, 8, unroll=2)
         def _(e):
             everyone = [id_rows[pl.ds(8 * r + e, 1), :] for r in range(6)]
             for k in range(first, first + count, 16):

time: 66.5 us -> 66.2 us (level)
  no operation moved by 1% of the time
where the time goes in v6:
time: 66.2 us; the launch traced here: 66 us
  Pallas kernels  62.4 us (94%)
  local copies, waits for them, and re-layouts  2.95 us (4%)
    pallas_call x1, Pallas kernels, per_device(): pl.pallas_call(kernel, out_shape=(out, out), in_specs=[pl.BlockSpec(memor...  62.4 us
    unnamed x2, local copies, waits for them, and re-layouts  2.95 us

profile of v6, /device:TPU:1, one launch (start us, length us, event | category | flops | bytes accessed | tf_op | source)
XLA Modules:
  0.0 66.0 jit_solution(11933540801332504763)
XLA Ops:
  0.6 62.4 %shard_map.86 = (f32[16,2,512]{2,1,0:T(2,128)}, f32[16,2,512]{2,1,0:T(2,128)}) custom-call(f32[16,2,512]{2,1,0:T(2,128)} %load_hbm.1, f32[2,512,512]{2,1,0:T(8,128)} %inverse_hbm.1, f32[2,512,512]{2,1,0:T(8,128)} %schur_hbm.1, f32[2,24,512]{2,1,0:T(8,128)} %map_hbm.1, s32[2,24]{1,0:T(2,128)} %ids_hbm.1, f32[24,72]{1,0:T(8,128)} %coarse_hbm.1, ...), custom_call_target="tpu_custom_call" | custom-call | tf_op jit(solution)/shard_map/pallas_call | solution.py:515
  63.1 1.5 %copy.11 = f32[16,2,512]{2,1,0:T(2,128)} copy(f32[16,2,512]{2,1,0:T(2,128)} %get-tuple-element.4) | data formatting | bytes 131072
  64.5 1.5 %copy.12 = f32[16,2,512]{2,1,0:T(2,128)} copy(f32[16,2,512]{2,1,0:T(2,128)} %get-tuple-element.5) | data formatting | bytes 131072
